TPU v7x, 32 devices: a whole 2x2x4 slice. The times are simulated.
32 devices in a mesh: dp: 8 (over y, x, core), mp: 4 (over z).
Axes of the slice: x: 2, y: 2, z: 4, core: 2. Of those that a mesh axis runs over, the one named last changes fastest.
Arguments:
- tokens: bfloat16 [16384, 768], P('dp'), may hold values from -6 to 6
- segments: int32 [16, 1024], P('dp'), may hold values from 0 to 7, never falling along the last dimension, each value on 1 to 512 neighbouring positions
- norm_gains: float32 [2, 768], replicated, may hold values from 0.1 to 1.9
- norm_shifts: float32 [2, 768], replicated, may hold values from -1.75 to 1.75
- qkv_weight: float32 [3, 768, 768], P(None, None, 'mp'), may hold values from -0.21875 to 0.21875
- qv_bias: float32 [2, 768], P(None, 'mp'), may hold values from -0.625 to 0.625
- out_weight: float32 [768, 768], P('mp'), may hold values from -1.75 to 1.75
- out_biases: float32 [2, 768], replicated, may hold values from -1.75 to 1.75
- up_weight: float32 [768, 3072], P(None, 'mp'), may hold values from -0.21875 to 0.21875
- up_bias: float32 [3072], P('mp'), may hold values from -3 to 3
- down_weight: float32 [3072, 768], P('mp'), may hold values from -0.109375 to 0.109375
- cotangent: bfloat16 [16384, 768], P('dp'), may hold values from -6 to 6
Outputs:
- result: bfloat16 [16384, 768], P('dp')
- token_grad: float32 [16384, 768], P('dp')
- gains_grad: float32 [2, 768], replicated
- shifts_grad: float32 [2, 768], replicated
- qkv_grad: float32 [3, 768, 768], P(None, None, 'mp')
- qv_bias_grad: float32 [2, 768], P(None, 'mp')
- out_weight_grad: float32 [768, 768], P('mp')
- out_biases_grad: float32 [2, 768], replicated
- up_grad: float32 [768, 3072], P(None, 'mp')
- up_bias_grad: float32 [3072], P('mp')
- down_grad: float32 [3072, 768], P('mp')
Inputs may be any that keep to these rules, and one draw needn't show every extreme that they name: `segments`: within each packed row the document numbers never fall, every number of 0 to 7 occurs, each document has 1 to 512 tokens, and some document has exactly 512.
All inputs are finite; a program needn't handle non-finite values.
Results may differ from a plain program's by a relative error of at most 0.012.
The roundings to bfloat16 on the way count: a program that leaves them out, or rounds other values in their place, can miss the bound.
Values sent between devices are 32-bit elements; how exact they have to be, the bound alone decides.
A program may use at most 192 MiB of HBM per device.

v0:
```python
from functools import partial

import jax
import jax.numpy as jnp
from jax import lax
from jax.experimental import pallas as pl
from jax.experimental.pallas import tpu as pltpu
from jax.sharding import PartitionSpec as P

F32 = jnp.float32
BF = jnp.bfloat16
HEAD_DIM = 64
NORM_EPSILON = 1e-06
BIG = 1e30
LOG2E = 1.4426950408889634
SAFE_SCORE = 60.0
REACH = 512
TILE = 256
LONG_TILE = 512
EXTRA = 16
UNIT = 256
EARLY = 2

NN = (((1,), (0,)), ((), ()))
NT = (((1,), (1,)), ((), ()))
TN = (((0,), (0,)), ((), ()))
WHOLE = pl.BlockSpec(memory_space=pltpu.VMEM)
ONCE = pl.BlockSpec(memory_space=pltpu.VMEM, pipeline_mode=pl.Buffered(1))
ANY = pl.BlockSpec(memory_space=pl.ANY)


def dot(left, right, dims):
    return lax.dot_general(left, right, dims, preferred_element_type=F32)


def params(mib=56):
    return pltpu.CompilerParams(vmem_limit_bytes=mib * 2**20)


def standardize(values):
    centered = values - jnp.mean(values, -1, keepdims=True)
    inv_std = lax.rsqrt(jnp.mean(centered * centered, -1, keepdims=True) + NORM_EPSILON)
    return centered * inv_std, inv_std


def norm_back(grad_in, normed, inv_std, gain):
    scaled = grad_in * gain
    return inv_std * (
        scaled
        - jnp.mean(scaled, -1, keepdims=True)
        - normed * jnp.mean(scaled * normed, -1, keepdims=True)
    )


def shape_of(shape, dtype):
    return jax.ShapeDtypeStruct(shape, dtype)


def flip(index, bit):
    return index + bit - 2 * bit * lax.rem(lax.div(index, bit), 2)


def remote(src, dst, send_sem, recv_sem, **where):
    return pltpu.make_async_remote_copy(
        src_ref=src, dst_ref=dst, send_sem=send_sem, recv_sem=recv_sem, device_id=where,
        device_id_type=pl.DeviceIdType.MESH,
    )


CORE, SIDE, ACROSS, DIAG_A, DIAG_B, CORE_SIDE, CORE_ACROSS, CORE_A, CORE_B = range(9)


class Spread:
    def __init__(self, piece, send_sems, recv_sems, mine=None):
        self.piece, self.send_sems, self.recv_sems, self.mine = piece, send_sems, recv_sems, mine
        self.device = lax.axis_index("dp")
        self.place = lax.rem(self.device, 8)

    def copy(self, chunk, kind, origin, bit, half=None, own=False):
        ref = self.piece(chunk, origin, half)
        return remote(
            self.mine(chunk) if own else ref, ref, self.send_sems.at[chunk, kind], self.recv_sems.at[chunk, kind], dp=flip(self.device, bit)
        )

    def origin(self, bits):
        place = self.place
        for bit in bits:
            place = flip(place, bit)
        return place

    def outgoing(self, chunk, kind):
        bits, bit, half = {
            CORE: ((), 1, None),
            SIDE: ((), 2, None),
            ACROSS: ((), 4, None),
            DIAG_A: ((2,), 4, 0),
            DIAG_B: ((4,), 2, 1),
            CORE_SIDE: ((2,), 1, None),
            CORE_ACROSS: ((4,), 1, None),
            CORE_A: ((2, 4), 1, 0),
            CORE_B: ((2, 4), 1, 1),
        }[kind]
        own = self.mine is not None and kind in (CORE, SIDE, ACROSS)
        return self.copy(chunk, kind, self.origin(bits), bit, half, own)

    def incoming(self, chunk, kind):
        bits, bit, half = {
            CORE: ((1,), 1, None),
            SIDE: ((2,), 2, None),
            ACROSS: ((4,), 4, None),
            DIAG_A: ((2, 4), 4, 0),
            DIAG_B: ((2, 4), 2, 1),
            CORE_SIDE: ((1, 2), 1, None),
            CORE_ACROSS: ((1, 4), 1, None),
            CORE_A: ((1, 2, 4), 1, 0),
            CORE_B: ((1, 2, 4), 1, 1),
        }[kind]
        return self.copy(chunk, kind, self.origin(bits), bit, half)

    def start(self, chunk, *kinds):
        for kind in kinds:
            self.outgoing(chunk, kind).start()

    def arrived(self, chunk, *kinds):
        for kind in kinds:
            self.incoming(chunk, kind).wait_recv()

    def send(self, chunk):
        self.start(chunk, SIDE, ACROSS, CORE)

    def forward(self, chunk):
        self.arrived(chunk, SIDE)
        self.start(chunk, DIAG_A, CORE_SIDE)
        self.arrived(chunk, ACROSS)
        self.start(chunk, DIAG_B, CORE_ACROSS)

    def corner(self, chunk):
        self.arrived(chunk, DIAG_A)
        self.start(chunk, CORE_A)
        self.arrived(chunk, DIAG_B)
        self.start(chunk, CORE_B)

    def complete(self, chunk):
        self.arrived(chunk, CORE, CORE_SIDE, CORE_ACROSS, CORE_A, CORE_B)

    def sent(self, chunk):
        for kind in range(9):
            self.outgoing(chunk, kind).wait_send()


def greet(*peers):
    barrier = pltpu.get_barrier_semaphore()
    for peer in peers:
        pl.semaphore_signal(barrier, inc=1, device_id=peer, device_id_type=pl.DeviceIdType.MESH)
    pl.semaphore_wait(barrier, len(peers))


def foreign_order(me):
    half = lax.div(me, 2)
    return flip(me, 1), 2 - half, 3 - 3 * half


def front_kernel(
    gain_ref, shift_ref, qkv_ref, out_ref, qv_bias_ref, up_bias_ref, seg_ref, x_any, up_any, down_any,
    smalls_ref, bound_ref, h1_out, w_out, wo_out, qkvt_out, ot_out, lse_out, land_out, z_out,
    x_in, h1_ref, land, wo_land, z_land, mlp_land, pieces, small_land, w_low, wo_low, bias_col,
    qkvt_ref, ot_ref, lse_ref, qx, kx, vx, kn,
    x_sem, piece_sems, keep_sems, out_sems, slice_sems, z_send, z_recv, own_send, small_send, small_recv,
    send_sems, recv_sems,
):
    parts, rows, width = land.shape
    own = out_ref.shape[0]
    heads = own // HEAD_DIM
    tokens = x_in.shape[0]
    length = seg_ref.shape[1]
    units = pieces.shape[0]
    items = 3 + units
    early = mlp_land.shape[0]
    share, out_share, mlp_share = rows // 8, own // 8, width // 8
    split = (0, share // 16 * 8 + 8, share)
    strip = UNIT // 8
    me = lax.axis_index("mp")
    device = lax.axis_index("dp")
    order = foreign_order(me)
    out_chunk, mlp_chunk = 2 * (parts - 1), 3 * (parts - 1)

    def slab_rows(h, origin, half=None):
        start, stop = split[h], split[h + 1]
        middle = start + (stop - start + 8) // 16 * 8
        if half is not None:
            start, stop = (start, middle) if half == 0 else (middle, stop)
        return pl.ds(pl.multiple_of(origin * share + start, 8), stop - start)

    def out_rows(origin, half=None):
        start, stop = {None: (0, out_share), 0: (0, 16), 1: (16, out_share)}[half]
        return pl.ds(pl.multiple_of(origin * out_share + start, 8), stop - start)

    def piece(c, origin, half):
        if c < out_chunk:
            return land.at[order[c // 2], slab_rows(c % 2, origin, half), :]
        if c < mlp_chunk:
            return wo_land.at[order[c - out_chunk], out_rows(origin, half), :]
        rows = pl.ds(pl.multiple_of(origin * mlp_share, 8), mlp_share)
        if half is None:
            return mlp_land.at[c - mlp_chunk, :, rows, :]
        return mlp_land.at[c - mlp_chunk, half, rows, :]

    def mine(c):
        if c < mlp_chunk:
            return piece(c, lax.rem(device, 8), None)
        return z_land.at[order[(c - mlp_chunk) // units], (c - mlp_chunk) % units]

    spread = Spread(piece, send_sems, recv_sems, mine)
    place = spread.place

    def hop_ref(source, item):
        if item < 2:
            return land.at[source, slab_rows(item, place), :]
        if item == 2:
            return wo_land.at[source, out_rows(place), :]
        return z_land.at[source, item - 3]

    def own_ref(item):
        if item < 2:
            return qkv_ref.at[slab_rows(item, place), :]
        if item == 2:
            return out_ref.at[out_rows(place), :]
        return pieces.at[item - 3]

    def own_copies(item, act):
        def copy(up):
            return remote(
                own_ref(item), hop_ref(me, item), own_send.at[item, up], z_recv.at[me, item], mp=me + 2 * up - 1
            )

        @pl.when(me < parts - 1)
        def _():
            act(copy(1))

        @pl.when(me > 0)
        def _():
            act(copy(0))

    def pass_on(j, item, act):
        source = order[j]
        ref = hop_ref(source, item)

        def copy(step):
            return remote(ref, ref, z_send.at[source, item], z_recv.at[source, item], mp=me + step)

        end = 0 if j < parts - 2 or item < 3 else 1

        @pl.when((source < me) & (me < parts - 1 - end))
        def _():
            act(copy(1))

        @pl.when((source > me) & (me > end))
        def _():
            act(copy(-1))

    def landed(j, item):
        ref = hop_ref(order[j], item)
        remote(ref, ref, z_send.at[order[j], item], z_recv.at[order[j], item], mp=me).wait_recv()
        pass_on(j, item, lambda copy: copy.start())
        if item >= 3 and j * units + item - 3 < early:
            keep(j * units + item - 3).start()

    inner = (me > 0) & (me < parts - 1)

    def landings(inner_items, outer_items):
        @pl.when(inner)
        def _():
            for j, item in inner_items:
                landed(j, item)

        @pl.when(jnp.logical_not(inner))
        def _():
            for j, item in outer_items:
                landed(j, item)

    def keep(c):
        return pltpu.make_async_copy(
            mine(mlp_chunk + c), piece(mlp_chunk + c, place, None), keep_sems.at[c]
        )

    def small_copy(s):
        ref = small_land.at[me]
        return remote(ref, ref, small_send.at[s - 1], small_recv.at[me], mp=lax.rem(me + s, parts))

    def at_place(at, ref):
        w_low[at] = ref[...].astype(BF)

    def slice_stores(at):
        rows_at = pl.ds(pl.multiple_of(at * rows, rows), rows)
        own_at = pl.ds(pl.multiple_of(at * own, own), own)
        return [
            pltpu.make_async_copy(w_low.at[at], w_out.at[rows_at, :], slice_sems.at[at, 0]),
            pltpu.make_async_copy(qkvt_ref.at[rows_at, :], qkvt_out.at[rows_at, :], slice_sems.at[at, 1]),
            pltpu.make_async_copy(ot_ref.at[own_at, :], ot_out.at[own_at, :], slice_sems.at[at, 2]),
        ]

    x_copy = pltpu.make_async_copy(x_any, x_in, x_sem)
    h1_copy = pltpu.make_async_copy(h1_ref, h1_out, out_sems.at[0])
    lse_copy = pltpu.make_async_copy(lse_ref, lse_out, out_sems.at[1])
    wo_copy = pltpu.make_async_copy(wo_low, wo_out, out_sems.at[2])
    z_copy = pltpu.make_async_copy(z_land, z_out, out_sems.at[3])
    land_copy = pltpu.make_async_copy(mlp_land, land_out, out_sems.at[4])

    x_copy.start()
    copies = []
    for u in range(units):
        at = pl.ds(pl.multiple_of(place * mlp_share, 8), mlp_share)
        copies.append((up_any.at[at, pl.ds(u * UNIT, UNIT)], pieces.at[u, 0]))
        for c in range(width // UNIT):
            at = pl.ds(pl.multiple_of(u * UNIT + place * strip, 8), strip)
            copies.append((down_any.at[at, pl.ds(c * UNIT, UNIT)], pieces.at[u, 1, pl.ds(c * strip, strip), :]))
    piece_copies = [pltpu.make_async_copy(a, b, piece_sems.at[i]) for i, (a, b) in enumerate(copies)]
    for copy in piece_copies:
        copy.start()
    greet(
        *[{"mp": lax.rem(me + s, parts)} for s in range(1, parts)],
        *[{"dp": flip(device, bit)} for bit in (1, 2, 4)],
    )
    for item in range(2):
        own_copies(item, lambda copy: copy.start())
    small_land[me] = jnp.zeros(small_land.shape[1:], F32)
    small_land[me, 0:2, :own] = qv_bias_ref[...]
    small_land[me, 2:3, :] = up_bias_ref[...].reshape(1, width)
    for s in range(1, parts):
        small_copy(s).start()
    own_copies(2, lambda copy: copy.start())
    bound_ref[...] = jnp.zeros_like(bound_ref)
    bias_col[...] = jnp.zeros_like(bias_col)
    lse_ref[...] = jnp.zeros_like(lse_ref)
    z_land[me] = jnp.zeros(z_land.shape[1:], F32)

    @pl.when(jnp.logical_not(inner))
    def _():
        z_land[order[2]] = jnp.zeros(z_land.shape[1:], F32)

    for j in range(2):
        bias_col[0, 2 * j * own : (2 * j + 1) * own, :] = small_land[me].T[:own, j : j + 1]
    at_place(0, qkv_ref)
    wo_low[:own, :] = out_ref[...].astype(BF)
    x_copy.wait()

    def norm_tile(i, carry):
        at = pl.ds(pl.multiple_of(i * TILE, TILE), TILE)
        normed, _ = standardize(x_in[at, :].astype(F32))
        h1_ref[at, :] = (normed * gain_ref[0:1, :] + shift_ref[0:1, :]).astype(BF)
        return carry

    lax.fori_loop(0, tokens // TILE, norm_tile, 0)
    h1_copy.start()
    row = lax.broadcasted_iota(jnp.int32, (EXTRA, length), 0)
    for u in range(heads):
        vx[u, HEAD_DIM:, :] = jnp.ones((EXTRA, length), BF)

    def norm_bound(ref, u):
        value = ref[u, :HEAD_DIM, :].astype(F32)
        return jnp.max(jnp.sum(value * value, 0, keepdims=True), 1, keepdims=True)

    def attend(at, r):
        tokens_r = pl.ds(pl.multiple_of(r * length, length), length)
        base = at * rows
        value = dot(w_low[at], h1_ref[tokens_r, :], NT) + bias_col[at]
        scale = HEAD_DIM**-0.5
        qkvt_ref[pl.ds(pl.multiple_of(base, own), own), tokens_r] = value[:own].astype(BF) * jnp.asarray(scale, BF)
        qkvt_ref[pl.ds(pl.multiple_of(base + own, own), 2 * own), tokens_r] = value[own:].astype(BF)
        same = row == seg_ref[pl.ds(r, 1), :]
        for u in range(heads):
            qx[u, HEAD_DIM:, :] = jnp.where(same | (row >= 8), 0.0, -BIG).astype(BF)
            kx[u, HEAD_DIM:, :] = jnp.where(same, 1.0, 0.0).astype(BF)
        for u in range(heads):
            for k, ref in enumerate((qx, kx, vx)):
                from_row = pl.multiple_of(base + k * own + u * HEAD_DIM, HEAD_DIM)
                ref[u, :HEAD_DIM, :] = qkvt_ref[pl.ds(from_row, HEAD_DIM), tokens_r]
            kn[u] = kx[u].T
            bound_ref[...] = jnp.maximum(bound_ref[...], norm_bound(qx, u) * norm_bound(kx, u))
            to_row = pl.ds(pl.multiple_of(at * own + u * HEAD_DIM, HEAD_DIM), HEAD_DIM)
            for t in range(length // TILE):
                low, high = max(0, t * TILE - REACH), min(length, (t + 1) * TILE + REACH)
                cols = slice(t * TILE, (t + 1) * TILE)
                to_cols = pl.ds(pl.multiple_of(r * length + t * TILE, TILE), TILE)
                probs = [
                    jnp.exp2(dot(kn[u, k : k + TILE, :], qx[u, :, cols], NN) * LOG2E).astype(BF)
                    for k in range(low, high, TILE)
                ]
                out = dot(vx[u, :, low:high], jnp.concatenate(probs, 0), NN)
                total = out[HEAD_DIM : HEAD_DIM + 1, :]
                ot_ref[to_row, to_cols] = (out[:HEAD_DIM, :] * (1.0 / total)).astype(BF)
                lse_ref[pl.ds(at * heads + u, 1), to_cols] = jnp.log(total)

    w, m = out_chunk, mlp_chunk

    def event(n):
        if n == 0:
            landings(((0, 0), (1, 0)), ((0, 0),))
            spread.send(0)
            landings(((0, 1), (1, 1)), ((0, 1),))
            spread.send(1)
        if n == 1:
            for copy in piece_copies:
                copy.wait()
            landings(((2, 0),), ((1, 0),))
            spread.send(2)
            spread.forward(0)
            landings(((2, 1),), ((1, 1),))
            spread.send(3)
            own_copies(3, lambda copy: copy.start())
            spread.forward(1)
        if n == 2:
            landings(((0, 2), (1, 2)), ((2, 0),))
            spread.send(4)
            spread.corner(0)
            spread.forward(2)
            landings((), ((2, 1),))
            spread.send(5)
            own_copies(4, lambda copy: copy.start())
            spread.corner(1)
            spread.forward(3)
            for s in range(1, parts):
                ref = small_land.at[lax.rem(me + s, parts)]
                remote(ref, ref, small_send.at[0], small_recv.at[lax.rem(me + s, parts)], mp=me).wait_recv()
            smalls_ref[...] = small_land[...]
            for j, source in enumerate(order):
                cols = small_land[source].T
                for k in range(2):
                    bias_col[1 + j, 2 * k * own : (2 * k + 1) * own, :] = cols[:own, k : k + 1]
            spread.complete(0)
            spread.complete(1)
            at_place(1, land.at[order[0]])
        if n == 3:
            landings(((2, 2), (0, 3), (1, 3)), ((0, 2),))
            spread.send(w)
            spread.corner(2)
            spread.forward(4)
            own_copies(5, lambda copy: copy.start())
            spread.corner(3)
            spread.forward(5)
        if n == 4:
            landings(((0, 4), (1, 4)), ((1, 2), (0, 3)))
            spread.send(w + 1)
            spread.send(m)
            spread.corner(4)
            spread.corner(5)
            spread.forward(w)
            spread.complete(2)
            spread.complete(3)
            at_place(2, land.at[order[1]])
        if n == 5:
            landings(((0, 5), (1, 5)), ((2, 2), (0, 4)))
            spread.send(w + 2)
            spread.send(m + 1)
            spread.corner(w)
            spread.forward(w + 1)
            spread.forward(m)
        if n == 6:
            landings(((2, 3), (2, 4)), ((0, 5), (1, 3)))
            spread.forward(w + 2)
            spread.corner(w + 1)
            spread.corner(m)
            spread.forward(m + 1)
            spread.complete(4)
            spread.complete(5)
            at_place(3, land.at[order[2]])
        if n == 7:
            landings(((2, 5),), ((1, 4),))
            spread.corner(w + 2)
            spread.corner(m + 1)
            spread.complete(w)
            spread.complete(m)
        if n == 8:
            landings((), ((1, 5),))
            z_copy.start()
            spread.complete(w + 1)
            spread.complete(w + 2)
            spread.complete(m + 1)
            for c in range(early):
                keep(c).wait()
            land_copy.start()
            for j in range(parts - 1):
                wo_low[(j + 1) * own : (j + 2) * own, :] = wo_land[order[j]].astype(BF)
            wo_copy.start()
            lse_copy.start()

    event(0)

    def step(n, carry):
        at, r = lax.div(n, 2), lax.rem(n, 2)
        attend(at, r)

        @pl.when(r == 1)
        def _():
            for copy in slice_stores(at):
                copy.start()

        for e in range(1, 9):
            @pl.when(n + 1 == e)
            def _():
                event(e)

        return carry

    lax.fori_loop(0, 2 * parts, step, 0)
    for c in range(mlp_chunk + early):
        spread.sent(c)
    for item in range(items):
        own_copies(item, lambda copy: copy.wait_send())
        for j in range(parts - 1):
            pass_on(j, item, lambda copy: copy.wait_send())
    for s in range(1, parts):
        small_copy(s).wait_send()
    for copy in (h1_copy, lse_copy, wo_copy, z_copy, land_copy):
        copy.wait()
    for at in range(parts):
        for copy in slice_stores(at):
            copy.wait()


def front(x, seg, gains, shifts, qkv, out, qv_bias, up_bias, up, down):
    tokens, width = x.shape
    length = seg.shape[1]
    rows = qkv.shape[0]
    own = out.shape[0]
    parts = width // own
    heads = own // HEAD_DIM
    units = up.shape[1] // UNIT
    chunks = 3 * (parts - 1) + EARLY
    wide = HEAD_DIM + EXTRA
    dma = pltpu.SemaphoreType.DMA
    return pl.pallas_call(
        front_kernel,
        in_specs=[WHOLE] * 7 + [ANY] * 3,
        out_specs=[WHOLE] * 2 + [ANY] * 8,
        out_shape=[
            shape_of((parts, 8, width), F32),
            shape_of((8, 128), F32),
            shape_of((tokens, width), BF),
            shape_of((parts * rows, width), BF),
            shape_of((width, width), BF),
            shape_of((parts * rows, tokens), BF),
            shape_of((width, tokens), BF),
            shape_of((16, tokens), F32),
            shape_of((EARLY, 2, width, UNIT), F32),
            shape_of((parts, units, 2, width // 8, UNIT), F32),
        ],
        scratch_shapes=[
            pltpu.VMEM((tokens, width), BF),
            pltpu.VMEM((tokens, width), BF),
            pltpu.VMEM((parts, rows, width), F32),
            pltpu.VMEM((parts, own, width), F32),
            pltpu.VMEM((parts, units, 2, width // 8, UNIT), F32),
            pltpu.VMEM((EARLY, 2, width, UNIT), F32),
            pltpu.VMEM((units, 2, width // 8, UNIT), F32),
            pltpu.VMEM((parts, 8, width), F32),
            pltpu.VMEM((parts, rows, width), BF),
            pltpu.VMEM((width, width), BF),
            pltpu.VMEM((parts, rows, 1), F32),
            pltpu.VMEM((parts * rows, tokens), BF),
            pltpu.VMEM((width, tokens), BF),
            pltpu.VMEM((16, tokens), F32),
            pltpu.VMEM((heads, wide, length), BF),
            pltpu.VMEM((heads, wide, length), BF),
            pltpu.VMEM((heads, wide, length), BF),
            pltpu.VMEM((heads, length, wide), BF),
            dma,
            dma((units * (1 + width // UNIT),)),
            dma((EARLY,)),
            dma((5,)),
            dma((parts, 3)),
            dma((parts, 3 + units)),
            dma((parts, 3 + units)),
            dma((3 + units, 2)),
            dma((parts - 1,)),
            dma((parts,)),
            dma((chunks, 9)),
            dma((chunks, 9)),
        ],
        compiler_params=pltpu.CompilerParams(vmem_limit_bytes=62 * 2**20, collective_id=0, has_side_effects=True),
        name="front",
    )(gains, shifts, qkv, out, qv_bias, up_bias, seg, x, up, down)


def repair_kernel(
    bound_ref, seg_ref, qkvt_any, ot_in, lse_in, ot_out, lse_out, qx, kx, vx, lse_row, sems,
):
    rows_here, length = seg_ref.shape
    parts = 4
    own = qkvt_any.shape[0] // (3 * parts)
    heads = parts * own // HEAD_DIM
    safe = jnp.max(bound_ref[...]) < SAFE_SCORE**2

    @pl.when(jnp.logical_not(safe))
    def _():
        row = lax.broadcasted_iota(jnp.int32, (EXTRA, length), 0)
        vx[HEAD_DIM:, :] = jnp.ones((EXTRA, length), BF)

        def move(copies):
            copies = [pltpu.make_async_copy(a, b, sems.at[i]) for i, (a, b) in enumerate(copies)]
            for copy in copies:
                copy.start()
            for copy in copies:
                copy.wait()

        def head(i, carry):
            r, h = lax.div(i, heads), lax.rem(i, heads)
            rows = pl.ds(pl.multiple_of(h * HEAD_DIM, HEAD_DIM), HEAD_DIM)
            tokens = pl.ds(pl.multiple_of(r * length, length), length)
            head_at = lax.div(h, heads // parts) * 3 * own + lax.rem(h, heads // parts) * HEAD_DIM
            same = row == seg_ref[pl.ds(r, 1), :]
            qx[HEAD_DIM:, :] = jnp.where(same | (row >= 8), 0.0, -BIG).astype(BF)
            kx[HEAD_DIM:, :] = jnp.where(same, 1.0, 0.0).astype(BF)
            move([
                (
                    qkvt_any.at[pl.ds(pl.multiple_of(head_at + k * own, HEAD_DIM), HEAD_DIM), tokens],
                    target.at[pl.ds(0, HEAD_DIM), :],
                )
                for k, target in enumerate((qx, kx, vx))
            ])

            @pl.when(h == 0)
            def _():
                lse_row[...] = jnp.zeros_like(lse_row)

            for t in range(length // TILE):
                cols = slice(t * TILE, (t + 1) * TILE)
                scores = dot(kx[...], qx[:, cols], TN)
                highest = jnp.max(scores, 0, keepdims=True)
                probs = jnp.exp2((scores - highest) * LOG2E).astype(BF)
                out = dot(vx[...], probs, NN)
                total = out[HEAD_DIM : HEAD_DIM + 1, :]
                qx[:HEAD_DIM, cols] = (out[:HEAD_DIM, :] * (1.0 / total)).astype(BF)
                lse_row[pl.ds(h, 1), cols] = jnp.log(total) + highest
            move([(qx.at[pl.ds(0, HEAD_DIM), :], ot_out.at[rows, tokens])])

            @pl.when(h == heads - 1)
            def _():
                move([(lse_row, lse_out.at[:, tokens])])

            return carry

        lax.fori_loop(0, rows_here * heads, head, 0)


def repair(bound, seg, qkvt, ot, lse):
    length = seg.shape[1]
    return pl.pallas_call(
        repair_kernel,
        in_specs=[WHOLE, WHOLE, ANY, ANY, ANY],
        out_specs=[ANY, ANY],
        out_shape=[shape_of(ot.shape, BF), shape_of(lse.shape, F32)],
        input_output_aliases={3: 0, 4: 1},
        scratch_shapes=[pltpu.VMEM((HEAD_DIM + EXTRA, length), BF)] * 3
        + [pltpu.VMEM((16, length), F32), pltpu.SemaphoreType.DMA((3,))],
        compiler_params=params(),
        name="repair",
    )(bound, seg, qkvt, ot, lse)


def split3(value):
    first = value.astype(BF)
    rest = value - first.astype(F32)
    second = rest.astype(BF)
    return first, second, (rest - second.astype(F32)).astype(BF)


class Total:
    def __init__(self, out, sends, recvs, near=None, side_land=None, across_land=None):
        self.out, self.near = out, near
        self.side_land, self.across_land, self.sends, self.recvs = side_land, across_land, sends, recvs
        self.device = lax.axis_index("dp")
        place = lax.rem(self.device, 8)
        self.half = out.shape[0] // 2
        self.part, self.piece = self.half // 4, self.half // 8
        bits = [lax.rem(lax.div(place, bit), 2) for bit in (1, 2, 4)]
        self.base = bits[0] * self.half
        self.away = (1 - bits[0]) * self.half
        self.one = self.base + bits[1] * self.part
        self.one_away = self.base + (1 - bits[1]) * self.part
        self.two = self.base + 2 * self.part + bits[2] * self.part
        self.two_away = self.base + 2 * self.part + (1 - bits[2]) * self.part
        self.one_piece = self.one + bits[2] * self.piece
        self.one_piece_away = self.one + (1 - bits[2]) * self.piece
        self.two_piece = self.two + bits[1] * self.piece
        self.two_piece_away = self.two + (1 - bits[1]) * self.piece

    def rows(self, start, count):
        return self.out.at[pl.ds(pl.multiple_of(start, 8), count), :]

    def copy(self, sem, bit, src, dst):
        return remote(src, dst, self.sends.at[sem], self.recvs.at[sem], dp=flip(self.device, bit))

    def over(self, sem, bit, start, count):
        ref = self.rows(start, count)
        return self.copy(sem, bit, ref, ref)

    def copies(self, stage):
        part, piece = self.part, self.piece
        first, second = pl.ds(0, part), pl.ds(part, piece)
        if stage == 0:
            return [self.copy(0, 1, self.rows(self.away, self.half), self.near)]
        if stage == 1:
            return [
                self.copy(1, 2, self.rows(self.one_away, part), self.side_land.at[first, :]),
                self.copy(2, 4, self.rows(self.two_away, part), self.across_land.at[first, :]),
            ]
        if stage == 2:
            return [
                self.copy(3, 4, self.rows(self.one_piece_away, piece), self.across_land.at[second, :]),
                self.copy(4, 2, self.rows(self.two_piece_away, piece), self.side_land.at[second, :]),
            ]
        if stage == 3:
            return [self.over(5, 4, self.one_piece, piece), self.over(6, 2, self.two_piece, piece)]
        if stage == 4:
            return [self.over(7, 2, self.one, part), self.over(8, 4, self.two, part)]
        return [self.over(9, 1, self.base, self.half)]

    def arrivals(self, stage):
        part, piece = self.part, self.piece
        if stage == 3:
            return [self.over(5, 4, self.one_piece_away, piece), self.over(6, 2, self.two_piece_away, piece)]
        if stage == 4:
            return [self.over(7, 2, self.one_away, part), self.over(8, 4, self.two_away, part)]
        if stage == 5:
            return [self.over(9, 1, self.away, self.half)]
        return self.copies(stage)

    def add(self, start, ref, at, count):
        step = 48 if count % 48 == 0 else 56

        def some(i, carry):
            rows = pl.ds(pl.multiple_of(start + i * step, 8), step)
            self.out[rows, :] += ref[pl.ds(pl.multiple_of(at + i * step, 8), step), :]
            return carry

        lax.fori_loop(0, count // step, some, 0)

    def finish(self, stage):
        for copy in self.copies(stage):
            copy.wait_send()
        for copy in self.arrivals(stage):
            copy.wait_recv()
        if stage == 0:
            self.add(self.base, self.near, 0, self.half)
        elif stage == 1:
            self.add(self.one, self.side_land, 0, self.part)
            self.add(self.two, self.across_land, 0, self.part)
        elif stage == 2:
            self.add(self.one_piece, self.across_land, self.part, self.piece)
            self.add(self.two_piece, self.side_land, self.part, self.piece)

    def start(self, stage):
        for copy in self.copies(stage):
            copy.start()

    @staticmethod
    def scratch(rows, width):
        dma = pltpu.SemaphoreType.DMA
        return [
            dma((10,)),
            dma((10,)),
            pltpu.VMEM((rows // 2, width), F32),
            pltpu.VMEM((rows // 8 + rows // 16, width), F32),
            pltpu.VMEM((rows // 8 + rows // 16, width), F32),
        ]


def attend_back_kernel(
    seg_ref, qkv_ref, ot_ref, dt_ref, lse_ref, h1_any, main_any, tail_any,
    dqkv_ref, main_out, rest_out,
    qx, kx, vx, dx, qn, dn, kn, acc, h1_ref, main_ref, rest_ref, whole_ref, in_sems, out_sems, main_send, main_recv, *comm,
):
    step = pl.program_id(0)
    own, length = ot_ref.shape
    width = h1_ref.shape[1]
    heads = own // HEAD_DIM
    tail_at = rest_ref.shape[0] - tail_any.shape[0]
    main = Total(main_ref, main_send, main_recv)
    rest = Total(rest_ref, *comm)
    whole = Total(whole_ref, *comm[:2])
    loads = [
        pltpu.make_async_copy(main_any.at[pl.ds(pl.multiple_of(at, 8), main.piece), :], main.rows(at, main.piece), sem)
        for at, sem in ((main.one_piece, in_sems.at[0]), (main.two_piece, in_sems.at[1]))
    ]
    loads.append(pltpu.make_async_copy(tail_any, rest_ref.at[pl.ds(tail_at, tail_any.shape[0]), :], in_sems.at[2]))
    loads.append(pltpu.make_async_copy(h1_any, h1_ref, in_sems.at[3]))
    stores = [
        pltpu.make_async_copy(main_ref, main_out, out_sems.at[0]),
        pltpu.make_async_copy(whole_ref, rest_out, out_sems.at[1]),
    ]

    @pl.when(step == 0)
    def _():
        for copy in loads:
            copy.start()
        greet(*[{"dp": flip(main.device, bit)} for bit in (1, 2, 4)])
        for copy in loads[:2]:
            copy.wait()
        main.start(3)

    @pl.when(step == 1)
    def _():
        main.finish(3)
        main.start(4)

    @pl.when(step == 3)
    def _():
        rest.finish(0)
        rest.start(1)
        main.finish(4)
        main.start(5)

    @pl.when(step == 4)
    def _():
        rest.finish(1)
        rest.start(2)

    @pl.when(step == 5)
    def _():
        rest.finish(2)
        for at in (rest.one_piece, rest.two_piece):
            rows = pl.ds(pl.multiple_of(at, 8), rest.piece)
            whole_ref[rows, :] = rest_ref[rows, :]
        whole.start(3)
        main.finish(5)
        stores[0].start()

    @pl.when(step == 6)
    def _():
        whole.finish(3)
        whole.start(4)

    @pl.when(step == 7)
    def _():
        whole.finish(4)
        whole.start(5)

    row = lax.broadcasted_iota(jnp.int32, (EXTRA, length), 0)
    same = row == seg_ref[pl.ds(jnp.where((step == 1) | (step >= 5), 1, 0), 1), :]
    key_extra = jnp.where(same | ((row >= 8) & (row < 11)), 1.0, 0.0).astype(BF)
    value_extra = jnp.where(row < 3, 1.0, 0.0).astype(BF)
    query_extra = jnp.where(same | (row >= 8), 0.0, -BIG)

    def three_rows(value, at):
        first, second, third = split3(value)
        out = jnp.where(row == at, first.astype(F32), 0.0)
        out = jnp.where(row == at + 1, second.astype(F32), out)
        return jnp.where(row == at + 2, third.astype(F32), out)

    head_at = jnp.where(step < 2, 0, lax.rem(step - 2, 3) + 1) * heads

    def head(u):
        rows = slice(u * HEAD_DIM, (u + 1) * HEAD_DIM)
        dq_rows, dk_rows, dv_rows = (slice(rows.start + k * own, rows.stop + k * own) for k in range(3))
        qx[u, :HEAD_DIM, :] = qkv_ref[dq_rows, :]
        kx[u, :HEAD_DIM, :] = qkv_ref[dk_rows, :]
        vx[u, :HEAD_DIM, :] = qkv_ref[dv_rows, :]
        dx[u, :HEAD_DIM, :] = dt_ref[rows, :]
        inner = jnp.sum(dt_ref[rows, :].astype(F32) * ot_ref[rows, :].astype(F32), 0, keepdims=True)
        log_sum = lse_ref[pl.ds(head_at + u, 1), :]
        qx[u, HEAD_DIM:, :] = (query_extra + three_rows(-log_sum, 8)).astype(BF)
        kx[u, HEAD_DIM:, :] = key_extra
        vx[u, HEAD_DIM:, :] = value_extra
        dx[u, HEAD_DIM:, :] = three_rows(-inner, 0).astype(BF)
        qn[u] = qx[u].T
        dn[u] = dx[u].T
        kn[u] = kx[u].T
        for t in range(length // TILE):
            low, high = max(0, t * TILE - REACH), min(length, (t + 1) * TILE + REACH)
            keys = slice(t * TILE, (t + 1) * TILE)
            probs, score_grads = [], []
            for q in range(low, high, TILE):
                prob = jnp.exp2(dot(qn[u, q : q + TILE, :], kx[u, :, keys], NN) * LOG2E)
                prob_grad = dot(dn[u, q : q + TILE, :], vx[u, :, keys], NN)
                probs.append(prob.astype(BF))
                score_grads.append((prob * prob_grad).astype(BF))
            probs = jnp.concatenate(probs, 0)
            score_grads = jnp.concatenate(score_grads, 0)
            dqkv_ref[dv_rows, keys] = dot(dx[u, :HEAD_DIM, low:high], probs, NN).astype(BF)
            dqkv_ref[dk_rows, keys] = dot(qx[u, :HEAD_DIM, low:high], score_grads, NN).astype(BF)
            part = dot(score_grads, kx[u, :HEAD_DIM, keys], NT)
            if t == 0:
                acc[u, low:high, :] = part
                if high < length:
                    acc[u, high:, :] = jnp.zeros((length - high, HEAD_DIM), F32)
            else:
                acc[u, low:high, :] += part
        dqkv_ref[dq_rows, :] = (acc[u] * HEAD_DIM**-0.5).T.astype(BF)

    for u in range(heads):
        head(u)

    def own_grads(tokens, add):
        part = dot(dqkv_ref[...], h1_ref[tokens, :], NN)
        rest_ref[: 3 * own, :] = rest_ref[: 3 * own, :] + part if add else part
        ones = jnp.ones((8, length), BF)
        for k in (0, 2):
            rows = slice(3 * own + k * 4, 3 * own + k * 4 + 8)
            part = dot(ones, dqkv_ref[k * own : (k + 1) * own, :], NT)
            rest_ref[rows, :own] = rest_ref[rows, :own] + part if add else part

    @pl.when(step == 0)
    def _():
        rest_ref[3 * own : tail_at, :] = jnp.zeros((tail_at - 3 * own, width), F32)
        loads[3].wait()
        own_grads(slice(0, length), False)

    @pl.when(step == 1)
    def _():
        own_grads(slice(length, 2 * length), True)
        loads[2].wait()
        rest.start(0)

    @pl.when(step == 7)
    def _():
        whole.finish(5)
        stores[1].start()
        for copy in stores:
            copy.wait()


def attend_back(seg, qkvt, ot, dt, lse, h1, main, tail):
    width, tokens = ot.shape
    _, length = seg.shape
    own = width // 4
    heads = own // HEAD_DIM
    wide = HEAD_DIM + EXTRA
    rest_rows = 3 * own + 64 + tail.shape[0]
    row_of = lambda s: jnp.where((s == 1) | (s >= 5), 1, 0)
    part_of = lambda s: jnp.where(s < 2, 0, lax.rem(s - 2, 3) + 1)
    block = pl.BlockSpec((own, length), lambda s: (part_of(s), row_of(s)))
    wide_block = pl.BlockSpec((3 * own, length), lambda s: (part_of(s), row_of(s)))
    dma = pltpu.SemaphoreType.DMA
    return pl.pallas_call(
        attend_back_kernel,
        grid=(8,),
        in_specs=[ONCE, wide_block, block, block]
        + [pl.BlockSpec((16, length), lambda s: (0, row_of(s))), ANY, ANY, ANY],
        out_specs=[wide_block, ANY, ANY],
        out_shape=[shape_of(qkvt.shape, BF), shape_of(main.shape, F32), shape_of((rest_rows, width), F32)],
        scratch_shapes=[pltpu.VMEM((heads, wide, length), BF)] * 4
        + [pltpu.VMEM((heads, length, wide), BF)] * 3
        + [
            pltpu.VMEM((heads, length, HEAD_DIM), F32),
            pltpu.VMEM((tokens, width), BF),
            pltpu.VMEM(main.shape, F32),
            pltpu.VMEM((rest_rows, width), F32),
            pltpu.VMEM((rest_rows, width), F32),
            dma((4,)),
            dma((2,)),
            dma((10,)),
            dma((10,)),
        ]
        + Total.scratch(rest_rows, width),
        compiler_params=pltpu.CompilerParams(vmem_limit_bytes=60 * 2**20, collective_id=2, has_side_effects=True),
        name="attend_back",
    )(seg, qkvt, ot, dt, lse, h1, main, tail)


def token_kernel(
    dqkv_ref, w_ref, x_ref, mg_ref, gain_ref, main_any, rest_any, result_any,
    tg_ref, sums_ref, down_ref, up_ref, out_ref, result_ref, qkv_ref,
    main_v, rest_v, result_v, in_sems, out_sems,
):
    step = pl.program_id(0)
    last = pl.num_programs(0) - 1
    ff = down_ref.shape[0]
    own = out_ref.shape[0]
    out_at = 3 * own + 64
    loads = [
        pltpu.make_async_copy(source, target, in_sems.at[i])
        for i, (source, target) in enumerate(((rest_any, rest_v), (main_any, main_v), (result_any, result_v)))
    ]
    stores = [
        pltpu.make_async_copy(source, target, out_sems.at[i])
        for i, (source, target) in enumerate((
            (main_v.at[pl.ds(0, ff), :], down_ref),
            (main_v.at[pl.ds(ff, up_ref.shape[0]), :], up_ref),
            (rest_v.at[pl.ds(out_at, own), :], out_ref),
            (result_v, result_ref),
            (rest_v.at[pl.ds(0, 3 * own), :], qkv_ref),
        ))
    ]

    @pl.when(step == 0)
    def _():
        for copy in loads:
            copy.start()
        sums_ref[...] = jnp.zeros_like(sums_ref)

    @pl.when(step == last - 1)
    def _():
        for copy in loads:
            copy.wait()
        for copy in stores:
            copy.start()

    hg = dot(dqkv_ref[...], w_ref[...], TN)
    normed, inv_std = standardize(x_ref[...].astype(F32))
    tg_ref[...] = mg_ref[...] + norm_back(hg, normed, inv_std, gain_ref[0:1, :])
    sums_ref[0:1, :] += jnp.sum(hg * normed, 0, keepdims=True)
    sums_ref[1:2, :] += jnp.sum(hg, 0, keepdims=True)

    @pl.when(step == last)
    def _():
        for copy in stores:
            copy.wait()


def token_back(dqkv, weights, x, mg, gains, main, rest, result, ff, own):
    tokens, width = x.shape
    row = pl.BlockSpec((LONG_TILE, width), lambda t: (t, 0))
    col = pl.BlockSpec((weights.shape[0], LONG_TILE), lambda t: (0, t))
    dma = pltpu.SemaphoreType.DMA
    return pl.pallas_call(
        token_kernel,
        grid=(tokens // LONG_TILE,),
        in_specs=[col, ONCE, row, row, ONCE, ANY, ANY, ANY],
        out_specs=[row, ONCE, ANY, ANY, ANY, ANY, ANY],
        out_shape=[
            shape_of((tokens, width), F32),
            shape_of((8, width), F32),
            shape_of((ff, width), F32),
            shape_of((width, ff), F32),
            shape_of((own, width), F32),
            shape_of((tokens, width), BF),
            shape_of((3 * own, width), F32),
        ],
        scratch_shapes=[
            pltpu.VMEM(main.shape, F32),
            pltpu.VMEM(rest.shape, F32),
            pltpu.VMEM((tokens, width), BF),
            dma((3,)),
            dma((5,)),
        ],
        compiler_params=params(),
        name="token_back",
    )(dqkv, weights, x, mg, gains, main, rest, result)


def sums_kernel(
    in_ref, rest_any, gains_ref, shifts_ref, biases_ref, qv_bias_ref, up_bias_ref,
    land, rows_v, rows_sem, sends, recvs, *, own, exchange,
):
    width = in_ref.shape[1]
    at = 4 * own + 64
    loads = [
        pltpu.make_async_copy(rest_any.at[pl.ds(low, 16), :], rows_v.at[i], rows_sem.at[i])
        for i, low in enumerate((3 * own, at))
    ]
    for copy in loads:
        copy.start()
    if exchange:
        device = lax.axis_index("dp")
        place = lax.rem(device, 8)
        others = []
        for bits in range(1, 8):
            other = device
            for bit in (1, 2, 4):
                if bits & bit:
                    other = flip(other, bit)
            others.append(other)
        greet(*[{"dp": other} for other in others])
        copies = [
            remote(in_ref, land.at[place], sends.at[i], recvs.at[place], dp=other) for i, other in enumerate(others)
        ]
        for copy in copies:
            copy.start()
        land[place] = in_ref[...]
    for copy in loads:
        copy.wait()
    small = rows_v[1]
    biases_ref[...] = small[BIAS_ONE : BIAS_TWO + 1, :]
    up_bias_ref[...] = small[UP_BIAS : UP_BIAS + 1, :]
    qv_bias_ref[0:1, :] = rows_v[0, 0:1, :own]
    qv_bias_ref[1:2, :] = rows_v[0, 8:9, :own]
    gains_ref[1:2, :] = small[GAIN_TWO : GAIN_TWO + 1, :]
    shifts_ref[1:2, :] = small[SHIFT_TWO : SHIFT_TWO + 1, :]
    if exchange:
        for other in others:
            peer = lax.rem(other, 8)
            remote(in_ref, land.at[peer], sends.at[0], recvs.at[peer], dp=other).wait_recv()
        sums = jnp.sum(land[...], 0)
    else:
        sums = in_ref[...]
    gains_ref[0:1, :] = sums[0:1, :]
    shifts_ref[0:1, :] = sums[1:2, :]
    if exchange:
        for copy in copies:
            copy.wait_send()


def add_sums(sums, rest, own, exchange):
    width = sums.shape[1]
    dma = pltpu.SemaphoreType.DMA
    options = dict(collective_id=3, has_side_effects=True) if exchange else {}
    return pl.pallas_call(
        partial(sums_kernel, own=own, exchange=exchange),
        in_specs=[WHOLE, ANY],
        out_specs=[WHOLE] * 5,
        out_shape=[
            shape_of((2, width), F32),
            shape_of((2, width), F32),
            shape_of((2, width), F32),
            shape_of((2, own), F32),
            shape_of((1, width), F32),
        ],
        scratch_shapes=[
            pltpu.VMEM((8,) + sums.shape, F32),
            pltpu.VMEM((2, 16, width), F32),
            dma((2,)),
            dma((7,)),
            dma((8,)),
        ],
        compiler_params=pltpu.CompilerParams(**options),
        name="add_sums",
    )(sums, rest)


GELU_C = 0.7978845608028654
GELU_A = 0.044715


def gelu_both(pre):
    square = pre * pre
    half = 0.5 + 0.5 * jnp.tanh(pre * (GELU_C + (GELU_C * GELU_A) * square))
    act = pre * half
    slope = half + act * (1.0 - half) * (2.0 * GELU_C + (6.0 * GELU_C * GELU_A) * square)
    return act, slope


GAIN_TWO, SHIFT_TWO, BIAS_ONE, BIAS_TWO, UP_BIAS = range(5)


def mlp_kernel(
    wo_ref, smalls_ref, bias_ref, gain_ref, shift_ref, x_any, ot_any, g_any, up_any, down_any, land_any, z_any,
    result_out, mg_out, dt_out, main_out, tail_out,
    land, z_far, wide_w, own_w, g_ref, h2_ref, dt_ref, mine_ref, main_ref, tail_ref, mixed_ref, res_ref, hg_ref,
    up_low, down_low, pre_s, ag_s,
    in_sems, w_sems, keep_sems, far_keep, far_send, far_recv, out_sems, tile_sems, send_sems, recv_sems, *comm,
):
    tokens, width = g_ref.shape
    parts = smalls_ref.shape[0]
    own = mine_ref.shape[0]
    ff = up_any.shape[1]
    units = ff // UNIT
    chunks = units * (parts - 1)
    late = land.shape[0]
    early = chunks - late
    share = z_any.shape[3]
    strip = UNIT // 8
    tiles = tokens // TILE
    me = lax.axis_index("mp")
    order = foreign_order(me)
    total = Total(main_ref, *comm)

    def source_of(c):
        j = lax.div(c, units)
        return jnp.where(j == 0, order[0], jnp.where(j == 1, order[1], order[2]))

    def piece(e, origin, half):
        rows = pl.ds(pl.multiple_of(origin * share, 8), share)
        if half is None:
            return land.at[e, :, rows, :]
        return land.at[e, half, rows, :]

    far_at = units * (parts - 2) - early

    def mine(e):
        if e >= far_at:
            return z_far.at[e - far_at]
        return z_any.at[order[(early + e) // units], (early + e) % units]

    inner = (me > 0) & (me < parts - 1)

    def far_copy(u):
        step = jnp.where(lax.div(me, 2) == 0, -1, 1)
        return remote(z_any.at[order[2], u], z_far.at[u], far_send.at[u], far_recv.at[u], mp=me + step)

    def far_local(u):
        return pltpu.make_async_copy(z_any.at[order[2], u], z_far.at[u], far_keep.at[u])

    def far(u):
        @pl.when(inner)
        def _():
            far_local(u).wait()

        @pl.when(jnp.logical_not(inner))
        def _():
            remote(z_far.at[u], z_far.at[u], far_send.at[u], far_recv.at[u], mp=me).wait_recv()

    spread = Spread(piece, send_sems, recv_sems, mine)

    def keep(e):
        return pltpu.make_async_copy(mine(e), piece(e, spread.place, None), keep_sems.at[e])

    def serve(n):
        for e in range(late):
            @pl.when(n == e)
            def _():
                if e >= far_at:
                    far(e - far_at)
                    keep(e).start()
                spread.send(e)

            @pl.when(n == e + 1)
            def _():
                spread.forward(e)

            @pl.when(n == e + 2)
            def _():
                spread.corner(e)

    def reduce(n):
        @pl.when(n == units)
        def _():
            total.start(0)

        @pl.when(n == units + 5)
        def _():
            total.finish(0)
            total.start(1)

        @pl.when(n == units + 8)
        def _():
            total.finish(1)
            total.start(2)

    def unit(bias, grads_at):
        def front(i):
            rows = slice(i * TILE, (i + 1) * TILE)
            pre_s[i % 2] = dot(h2_ref[rows, :], up_low[...], NN) + bias
            ag_s[i % 2] = dot(g_ref[rows, :], down_low[...], NT)

        def back(i):
            rows = slice(i * TILE, (i + 1) * TILE)
            act, slope = gelu_both(pre_s[i % 2])
            act = act.astype(BF)
            pre_grad = (ag_s[i % 2] * slope).astype(BF)
            res_ref[rows, :] += dot(act, down_low[...], NN)
            hg_ref[rows, :] += dot(pre_grad, up_low[...], NT)
            if grads_at is not None:
                h2 = h2_ref[rows, :]
                g = g_ref[rows, :]
                cols = pl.ds(pl.multiple_of(grads_at, UNIT), UNIT)
                main_ref[cols, :] += dot(act, g, TN)
                main_ref[ff:, cols] += dot(h2, pre_grad, TN)
                at = own + UP_BIAS
                tail_ref[at : at + 1, cols] += jnp.sum(pre_grad.astype(F32), 0, keepdims=True)

        front(0)
        for i in range(tiles):
            if i + 1 < tiles:
                front(i + 1)
            back(i)

    loads = [
        pltpu.make_async_copy(source, target, in_sems.at[i])
        for i, (source, target) in enumerate(((ot_any, dt_ref), (x_any, h2_ref), (g_any, g_ref)))
    ]

    def own_load(u):
        cols = pl.ds(pl.multiple_of(u * UNIT, UNIT), UNIT)
        return [
            pltpu.make_async_copy(up_any.at[:, cols], wide_w.at[0], w_sems.at[0]),
            pltpu.make_async_copy(down_any.at[cols, :], own_w, w_sems.at[1]),
        ]

    def chunk_load(c):
        return pltpu.make_async_copy(land_any.at[c], wide_w, w_sems.at[0])

    for copy in loads:
        copy.start()
    for copy in own_load(0):
        copy.start()
    for e in range(far_at):
        keep(e).start()

    @pl.when(inner)
    def _():
        for u in range(units):
            far_local(u).start()

    greet(
        *[{"mp": lax.rem(me + s, parts)} for s in range(1, parts)],
        *[{"dp": flip(spread.device, bit)} for bit in (1, 2, 4)],
    )

    @pl.when(inner)
    def _():
        for u in range(units):
            far_copy(u).start()

    serve(0)
    main_ref[...] = jnp.zeros_like(main_ref)
    tail_ref[...] = jnp.zeros_like(tail_ref)
    for copy in loads[:2]:
        copy.wait()
    mine_ref[...] = dt_ref[:own, :]

    def first(i, carry):
        rows = pl.ds(pl.multiple_of(i * TILE, TILE), TILE)
        mixed = h2_ref[rows, :].astype(F32) + dot(dt_ref[:, rows], wo_ref[...], TN) + bias_ref[0:1, :]
        mixed_ref[rows, :] = mixed
        res_ref[rows, :] = mixed + bias_ref[1:2, :]
        hg_ref[rows, :] = jnp.zeros((TILE, width), F32)
        normed, _ = standardize(mixed)
        h2_ref[rows, :] = (normed * gain_ref[1:2, :] + shift_ref[1:2, :]).astype(BF)
        return carry

    lax.fori_loop(0, tiles, first, 0)
    loads[2].wait()

    def own_unit(u, carry):
        for copy in own_load(u):
            copy.wait()
        up_low[...] = wide_w[0].astype(BF)
        down_low[...] = own_w[...].astype(BF)

        @pl.when(u + 1 < units)
        def _():
            for copy in own_load(u + 1):
                copy.start()

        @pl.when(u + 1 == units)
        def _():
            chunk_load(0).start()

        unit(smalls_ref[me, 2:3, pl.ds(pl.multiple_of(u * UNIT, UNIT), UNIT)], u * UNIT)
        serve(u + 1)
        reduce(u + 1)
        return carry

    lax.fori_loop(0, units, own_unit, 0)

    def take(ref, at):
        up_low[...] = ref[at + (0,)].astype(BF)
        for q in range(8):
            for k in range(width // UNIT):
                low = q * share + k * strip
                down_low[q * strip : (q + 1) * strip, k * UNIT : (k + 1) * UNIT] = ref[
                    at + (1, slice(low, low + strip))
                ].astype(BF)

    def foreign_unit(c, carry):
        @pl.when(c < early)
        def _():
            chunk_load(c).wait()
            take(wide_w, ())

        @pl.when(c + 1 < early)
        def _():
            chunk_load(c + 1).start()

        @pl.when(c >= early)
        def _():
            e = c - early
            pltpu.make_async_copy(z_far.at[0], piece(e, spread.place, None), keep_sems.at[e]).wait()
            spread.complete(e)
            take(land, (e,))

        cols = pl.ds(pl.multiple_of(lax.rem(c, units) * UNIT, UNIT), UNIT)
        unit(smalls_ref[source_of(c), 2:3, cols], None)
        serve(c + units + 1)
        reduce(c + units + 1)
        return carry

    lax.fori_loop(0, chunks, foreign_unit, 0)

    def tile_stores(i):
        rows = pl.ds(pl.multiple_of(i * TILE, TILE), TILE)
        return [
            pltpu.make_async_copy(source, target, tile_sems.at[i, k])
            for k, (source, target) in enumerate((
                (h2_ref.at[rows, :], result_out.at[rows, :]),
                (hg_ref.at[rows, :], mg_out.at[rows, :]),
                (dt_ref.at[:, rows], dt_out.at[:, rows]),
            ))
        ]

    def finish(i, carry):
        rows = pl.ds(pl.multiple_of(i * TILE, TILE), TILE)
        g = g_ref[rows, :].astype(F32)
        h2_ref[rows, :] = res_ref[rows, :].astype(BF)
        normed, inv_std = standardize(mixed_ref[rows, :])
        hg = hg_ref[rows, :]
        mg = g + norm_back(hg, normed, inv_std, gain_ref[1:2, :])
        hg_ref[rows, :] = mg
        low = mg.astype(BF)
        dt_ref[:, rows] = dot(wo_ref[...], low, NT).astype(BF)
        tail_ref[:own, :] += dot(mine_ref[:, rows], low, NN)
        for at, value in ((GAIN_TWO, hg * normed), (SHIFT_TWO, hg), (BIAS_ONE, mg), (BIAS_TWO, g)):
            tail_ref[own + at : own + at + 1, :] += jnp.sum(value, 0, keepdims=True)
        for copy in tile_stores(i):
            copy.start()
        return carry

    lax.fori_loop(0, tiles, finish, 0)
    total.finish(2)
    ends = [
        pltpu.make_async_copy(total.rows(at, total.piece), main_out.at[pl.ds(pl.multiple_of(at, 8), total.piece), :], sem)
        for at, sem in ((total.one_piece, out_sems.at[0]), (total.two_piece, out_sems.at[1]))
    ]
    ends.append(pltpu.make_async_copy(tail_ref, tail_out, out_sems.at[2]))
    for copy in ends:
        copy.start()
    for e in range(late):
        spread.sent(e)

    @pl.when(inner)
    def _():
        for u in range(units):
            far_copy(u).wait_send()

    def drain(i, carry):
        for copy in tile_stores(i):
            copy.wait()
        return carry

    lax.fori_loop(0, tiles, drain, 0)
    for copy in ends:
        copy.wait()


def mlp(x, ot, wo, g, up, down, smalls, biases, gains, shifts, land, z):
    tokens, width = x.shape
    parts = smalls.shape[0]
    own = width // parts
    ff = up.shape[1]
    units = ff // UNIT
    chunks = units * (parts - 1)
    late = chunks - land.shape[0]
    tiles = tokens // TILE
    rows = 2 * ff
    tail = own + 64
    dma = pltpu.SemaphoreType.DMA
    return pl.pallas_call(
        mlp_kernel,
        in_specs=[WHOLE] * 5 + [ANY] * 7,
        out_specs=[ANY] * 5,
        out_shape=[
            shape_of((tokens, width), BF),
            shape_of((tokens, width), F32),
            shape_of((width, tokens), BF),
            shape_of((rows, width), F32),
            shape_of((tail, width), F32),
        ],
        scratch_shapes=[
            pltpu.VMEM((late, 2, width, UNIT), F32),
            pltpu.VMEM((units, 2, width // 8, UNIT), F32),
            pltpu.VMEM((2, width, UNIT), F32),
            pltpu.VMEM((UNIT, width), F32),
            pltpu.VMEM((tokens, width), BF),
            pltpu.VMEM((tokens, width), BF),
            pltpu.VMEM((width, tokens), BF),
            pltpu.VMEM((own, tokens), BF),
            pltpu.VMEM((rows, width), F32),
            pltpu.VMEM((tail, width), F32),
            pltpu.VMEM((tokens, width), F32),
            pltpu.VMEM((tokens, width), F32),
            pltpu.VMEM((tokens, width), F32),
            pltpu.VMEM((width, UNIT), BF),
            pltpu.VMEM((UNIT, width), BF),
            pltpu.VMEM((2, TILE, UNIT), F32),
            pltpu.VMEM((2, TILE, UNIT), F32),
            dma((3,)),
            dma((2,)),
            dma((late,)),
            dma((units,)),
            dma((units,)),
            dma((units,)),
            dma((3,)),
            dma((tiles, 3)),
            dma((late, 9)),
            dma((late, 9)),
        ]
        + Total.scratch(rows, width),
        compiler_params=pltpu.CompilerParams(vmem_limit_bytes=63 * 2**20, collective_id=1, has_side_effects=True),
        name="mlp",
    )(wo, smalls, biases, gains, shifts, x, ot, g, up, down, land, z)


def body(
    dp_size,
    tokens,
    segments,
    norm_gains,
    norm_shifts,
    qkv_weight,
    qv_bias,
    out_weight,
    out_biases,
    up_weight,
    up_bias,
    down_weight,
    cotangent,
):
    width = tokens.shape[1]
    own = qkv_weight.shape[2]
    ff = up_weight.shape[1]
    smalls, bound, h1, weights, wo, qkvt, ot, lse, land, z = front(
        tokens, segments, norm_gains, norm_shifts, qkv_weight.transpose(0, 2, 1).reshape(3 * own, width), out_weight,
        qv_bias, up_bias, up_weight, down_weight,
    )
    ot, lse = repair(bound, segments, qkvt, ot, lse)
    result, mg, dt, main, tail = mlp(
        tokens, ot, wo, cotangent, up_weight, down_weight, smalls, out_biases, norm_gains, norm_shifts, land, z
    )
    dqkv, main, rest = attend_back(segments, qkvt, ot, dt, lse, h1, main, tail)
    if dp_size > 8:
        main, rest = (value / 8 for value in lax.psum((main, rest), "dp"))
    token_grad, sums_one, down_grad, up_grad, out_weight_grad, result, qkv_grad = token_back(
        dqkv, weights, tokens, mg, norm_gains, main, rest, result, ff, own
    )
    if dp_size > 8:
        sums_one = lax.psum(sums_one, "dp")
    gains_grad, shifts_grad, out_biases_grad, qv_bias_grad, up_bias_grad = add_sums(sums_one, rest, own, dp_size == 8)
    return (
        result,
        token_grad,
        gains_grad,
        shifts_grad,
        qkv_grad.reshape(3, own, width).transpose(0, 2, 1),
        qv_bias_grad,
        out_weight_grad,
        out_biases_grad,
        up_grad,
        up_bias_grad.reshape(ff),
        down_grad,
    )


def solution(mesh):
    in_specs = (
        P("dp", None),
        P("dp", None),
        P(),
        P(),
        P(None, None, "mp"),
        P(None, "mp"),
        P("mp", None),
        P(),
        P(None, "mp"),
        P("mp"),
        P("mp", None),
        P("dp", None),
    )
    out_specs = (
        P("dp", None),
        P("dp", None),
        P(),
        P(),
        P(None, None, "mp"),
        P(None, "mp"),
        P("mp", None),
        P(),
        P(None, "mp"),
        P("mp"),
        P("mp", None),
    )
    return jax.shard_map(
        partial(body, mesh.shape["dp"]), mesh=mesh, in_specs=in_specs, out_specs=out_specs, check_vma=False
    )
```

profile of v0, /device:TPU:0, one launch (start us, length us, event | category | flops | bytes accessed | tf_op | source)
XLA Modules:
  0.0 266.8 jit_solution(14229277124073727287)
XLA Ops:
  0.6 72.3 %front.1 = (f32[4,8,768]{2,1,0:T(8,128)}, f32[8,128]{1,0:T(8,128)}, bf16[2048,768]{1,0:T(8,128)(2,1)}, bf16[2304,768]{1,0:T(8,128)(2,1)}, bf16[768,768]{1,0:T(8,...) custom-call(f32[2,768]{1,0:T(2,128)} %gain_ref.5, ...), custom_call_target="tpu_custom_call" | custom-call | tf_op jit(solution)/shard_map/front/pallas_call | solution.py:532
  72.9 0.9 repair.1
  73.8 94.7 %mlp.1 = (bf16[2048,768]{1,0:T(8,128)(2,1)}, f32[2048,768]{1,0:T(8,128)}, bf16[768,2048]{1,0:T(8,128)(2,1)}, f32[1536,768]{1,0:T(8,128)}, f32[256,768]{1,0:T(8,128)}) custom-call(bf16[768,768]{1,0:T(8,128)(2,1)} %get-tuple-element.48.wo_ref, f32[4,8,768]{2,1,0:T(8,128)} %get-tuple-element.49.smalls_ref, f32[2,768]{1,0:T(2,128)} %bias_ref.1, ...), custom_call_target="tpu_custom_call" | custom-call | tf_op jit(solution)/shard_map/mlp/pallas_call | solution.py:1438
  168.5 67.1 %attend_back.1 = (bf16[2304,2048]{1,0:T(8,128)(2,1)}, f32[1536,768]{1,0:T(8,128)}, f32[896,768]{1,0:T(8,128)}) custom-call(s32[2,1024]{1,0:T(2,128)} %seg_ref.5, bf16[2304,2048]{1,0:T(8,128)(2,1)} %get-tuple-element.43.qkvt_any.qkv_ref, bf16[768,2048]{1,0:T(8,128)(2,1)} %get-tuple-element.47.ot_any.ot_ref, bf16[768,2048]{1,0:T(8,128)(2,1)} %get-tuple-element.52.dt_ref, ...), custom_call_target="tpu_custom_call" | custom-call | tf_op jit(solution)/shard_map/attend_back/pallas_call | solution.py:935
  235.6 17.5 %token_back.1 = (f32[2048,768]{1,0:T(8,128)}, f32[8,768]{1,0:T(8,128)}, f32[768,768]{1,0:T(8,128)}, f32[768,768]{1,0:T(8,128)}, f32[192,768]{1,0:T(8,128)}, /*in...) custom-call(bf16[2304,2048]{1,0:T(8,128)(2,1)} %get-tuple-element.57.dqkv_ref, bf16[2304,768]{1,0:T(8,128)(2,1)} %get-tuple-element.58.w_ref, ...), custom_call_target="tpu_custom_call" | custom-call | tf_op jit(solution)/shard_map/token_back/pallas_call | solution.py:1016
  253.2 7.3 %add_sums.1 = (f32[2,768]{1,0:T(2,128)}, f32[2,768]{1,0:T(2,128)}, f32[2,768]{1,0:T(2,128)}, f32[2,192]{1,0:T(2,128)}, f32[1,768]{1,0:T(1,128)}) custom-call(f32[8,768]{1,0:T(8,128)} %get-tuple-element.65.in_ref, f32[896,768]{1,0:T(8,128)} %get-tuple-element.61.rest_any), custom_call_target="tpu_custom_call" | custom-call | tf_op jit(solution)/shard_map/add_sums/pallas_call | solution.py:1098
  260.5 1.3 reduce
  261.8 1.3 copy.31
  263.1 1.3 copy.32
  264.3 1.2 copy.33
  265.5 1.3 copy.34
where the time goes:
time: 267 us
  Pallas kernels  260 us (97%)
  local copies, waits for them, and re-layouts  5.05 us (2%)
    pallas_call x1, Pallas kernels, mlp(): pl.pallas_call(mlp_kernel, in_specs=[WHOLE] * 5 + [ANY] * 7, out_specs=[A...  94.7 us
    pallas_call x1, Pallas kernels, front(): pl.pallas_call(front_kernel, in_specs=[WHOLE] * 7 + [ANY] * 3, out_specs=...  72.3 us
    pallas_call x1, Pallas kernels, attend_back(): pl.pallas_call(attend_back_kernel, grid=(8,), in_specs=[ONCE, wide_block,...  67.1 us
    pallas_call x1, Pallas kernels, token_back(): pl.pallas_call(token_kernel, grid=(tokens // LONG_TILE,), in_specs=[col,...  17.5 us
    pallas_call x1, Pallas kernels, add_sums(): pl.pallas_call(partial(sums_kernel, own=own, exchange=exchange), in_specs...  7.33 us

commit v1 on v0

--- a/solution.py
+++ b/solution.py
@@ -19,7 +19,7 @@
 LONG_TILE = 512
 EXTRA = 16
 UNIT = 256
-EARLY = 2
+EARLY = 1
 
 NN = (((1,), (0,)), ((), ()))
 NT = (((1,), (1,)), ((), ()))
@@ -67,85 +67,62 @@
     )
 
 
-CORE, SIDE, ACROSS, DIAG_A, DIAG_B, CORE_SIDE, CORE_ACROSS, CORE_A, CORE_B = range(9)
+SIDE, ACROSS, DIAG_A, DIAG_B, CORE = range(5)
+NEAR, CORNER, OTHER = range(3)
+
+
+def position(device):
+    place = lax.rem(device, 8)
+    return lax.rem(place, 2) * 4 + lax.div(place, 2)
 
 
 class Spread:
-    def __init__(self, piece, send_sems, recv_sems, mine=None):
-        self.piece, self.send_sems, self.recv_sems, self.mine = piece, send_sems, recv_sems, mine
+    def __init__(self, pieces, send_sems, recv_sems, mine=None):
+        self.pieces, self.send_sems, self.recv_sems, self.mine = pieces, send_sems, recv_sems, mine
         self.device = lax.axis_index("dp")
-        self.place = lax.rem(self.device, 8)
-
-    def copy(self, chunk, kind, origin, bit, half=None, own=False):
-        ref = self.piece(chunk, origin, half)
+        self.at = position(self.device)
+        self.side, self.across = flip(self.at, 1), flip(self.at, 2)
+        self.corner_at = flip(self.side, 2)
+        self.core = lax.div(self.at, 4) * 4
+
+    def copy(self, chunk, kind, src=None):
+        at, count, half, bit, arrival = {
+            SIDE: (self.at, 1, None, 2, NEAR),
+            ACROSS: (self.at, 1, None, 4, NEAR),
+            DIAG_A: (self.side, 1, 0, 4, CORNER),
+            DIAG_B: (self.across, 1, 1, 2, CORNER),
+            CORE: (self.core, 4, None, 1, OTHER),
+        }[kind]
+        dst = self.pieces(chunk, at, count, half)
         return remote(
-            self.mine(chunk) if own else ref, ref, self.send_sems.at[chunk, kind], self.recv_sems.at[chunk, kind], dp=flip(self.device, bit)
+            dst if src is None else src, dst, self.send_sems.at[chunk], self.recv_sems.at[chunk, arrival],
+            dp=flip(self.device, bit),
         )
 
-    def origin(self, bits):
-        place = self.place
-        for bit in bits:
-            place = flip(place, bit)
-        return place
-
-    def outgoing(self, chunk, kind):
-        bits, bit, half = {
-            CORE: ((), 1, None),
-            SIDE: ((), 2, None),
-            ACROSS: ((), 4, None),
-            DIAG_A: ((2,), 4, 0),
-            DIAG_B: ((4,), 2, 1),
-            CORE_SIDE: ((2,), 1, None),
-            CORE_ACROSS: ((4,), 1, None),
-            CORE_A: ((2, 4), 1, 0),
-            CORE_B: ((2, 4), 1, 1),
-        }[kind]
-        own = self.mine is not None and kind in (CORE, SIDE, ACROSS)
-        return self.copy(chunk, kind, self.origin(bits), bit, half, own)
-
-    def incoming(self, chunk, kind):
-        bits, bit, half = {
-            CORE: ((1,), 1, None),
-            SIDE: ((2,), 2, None),
-            ACROSS: ((4,), 4, None),
-            DIAG_A: ((2, 4), 4, 0),
-            DIAG_B: ((2, 4), 2, 1),
-            CORE_SIDE: ((1, 2), 1, None),
-            CORE_ACROSS: ((1, 4), 1, None),
-            CORE_A: ((1, 2, 4), 1, 0),
-            CORE_B: ((1, 2, 4), 1, 1),
-        }[kind]
-        return self.copy(chunk, kind, self.origin(bits), bit, half)
-
-    def start(self, chunk, *kinds):
-        for kind in kinds:
-            self.outgoing(chunk, kind).start()
-
-    def arrived(self, chunk, *kinds):
-        for kind in kinds:
-            self.incoming(chunk, kind).wait_recv()
+    def arrived(self, chunk, arrival, count):
+        ref = self.pieces(chunk, 0, count, None)
+        remote(ref, ref, self.send_sems.at[chunk], self.recv_sems.at[chunk, arrival], dp=self.device).wait_recv()
 
     def send(self, chunk):
-        self.start(chunk, SIDE, ACROSS, CORE)
+        src = None if self.mine is None else self.mine(chunk)
+        for kind in (SIDE, ACROSS):
+            self.copy(chunk, kind, src).start()
 
     def forward(self, chunk):
-        self.arrived(chunk, SIDE)
-        self.start(chunk, DIAG_A, CORE_SIDE)
-        self.arrived(chunk, ACROSS)
-        self.start(chunk, DIAG_B, CORE_ACROSS)
+        self.arrived(chunk, NEAR, 2)
+        for kind in (DIAG_A, DIAG_B):
+            self.copy(chunk, kind).start()
 
     def corner(self, chunk):
-        self.arrived(chunk, DIAG_A)
-        self.start(chunk, CORE_A)
-        self.arrived(chunk, DIAG_B)
-        self.start(chunk, CORE_B)
+        self.arrived(chunk, CORNER, 1)
+        self.copy(chunk, CORE).start()
 
     def complete(self, chunk):
-        self.arrived(chunk, CORE, CORE_SIDE, CORE_ACROSS, CORE_A, CORE_B)
+        self.arrived(chunk, OTHER, 4)
 
     def sent(self, chunk):
-        for kind in range(9):
-            self.outgoing(chunk, kind).wait_send()
+        ref = self.pieces(chunk, 0, 7, None)
+        remote(ref, ref, self.send_sems.at[chunk], self.recv_sems.at[chunk, 0], dp=self.device).wait_send()
 
 
 def greet(*peers):
@@ -165,7 +142,7 @@
     smalls_ref, bound_ref, h1_out, w_out, wo_out, qkvt_out, ot_out, lse_out, land_out, z_out,
     x_in, h1_ref, land, wo_land, z_land, mlp_land, pieces, small_land, w_low, wo_low, bias_col,
     qkvt_ref, ot_ref, lse_ref, qx, kx, vx, kn,
-    x_sem, piece_sems, keep_sems, out_sems, slice_sems, z_send, z_recv, own_send, small_send, small_recv,
+    x_sem, piece_sem, keep_sems, out_sems, slice_sems, z_send, z_recv, own_send, small_send, small_recv,
     send_sems, recv_sems,
 ):
     parts, rows, width = land.shape
@@ -184,34 +161,37 @@
     order = foreign_order(me)
     out_chunk, mlp_chunk = 2 * (parts - 1), 3 * (parts - 1)
 
-    def slab_rows(h, origin, half=None):
-        start, stop = split[h], split[h + 1]
-        middle = start + (stop - start + 8) // 16 * 8
+    def some_rows(start, size, at, count, half):
+        low, high = 0, count * size
         if half is not None:
-            start, stop = (start, middle) if half == 0 else (middle, stop)
-        return pl.ds(pl.multiple_of(origin * share + start, 8), stop - start)
-
-    def out_rows(origin, half=None):
-        start, stop = {None: (0, out_share), 0: (0, 16), 1: (16, out_share)}[half]
-        return pl.ds(pl.multiple_of(origin * out_share + start, 8), stop - start)
-
-    def piece(c, origin, half):
+            middle = (size + 8) // 16 * 8
+            low, high = (0, middle) if half == 0 else (middle, size)
+        return pl.ds(pl.multiple_of(start + at * size + low, 8), high - low)
+
+    def slab_rows(h, at, count=1, half=None):
+        return some_rows(split[h] * 8, split[h + 1] - split[h], at, count, half)
+
+    def out_rows(at, count=1, half=None):
+        return some_rows(0, out_share, at, count, half)
+
+    def pieces_at(c, at, count, half):
         if c < out_chunk:
-            return land.at[order[c // 2], slab_rows(c % 2, origin, half), :]
+            return land.at[order[c // 2], slab_rows(c % 2, at, count, half), :]
         if c < mlp_chunk:
-            return wo_land.at[order[c - out_chunk], out_rows(origin, half), :]
-        rows = pl.ds(pl.multiple_of(origin * mlp_share, 8), mlp_share)
+            return wo_land.at[order[c - out_chunk], out_rows(at, count, half), :]
+        rows = some_rows(0, mlp_share, at, count, None)
         if half is None:
             return mlp_land.at[c - mlp_chunk, :, rows, :]
         return mlp_land.at[c - mlp_chunk, half, rows, :]
 
+    place = position(device)
+
     def mine(c):
         if c < mlp_chunk:
-            return piece(c, lax.rem(device, 8), None)
+            return pieces_at(c, place, 1, None)
         return z_land.at[order[(c - mlp_chunk) // units], (c - mlp_chunk) % units]
 
-    spread = Spread(piece, send_sems, recv_sems, mine)
-    place = spread.place
+    spread = Spread(pieces_at, send_sems, recv_sems, mine)
 
     def hop_ref(source, item):
         if item < 2:
@@ -248,7 +228,7 @@
         def copy(step):
             return remote(ref, ref, z_send.at[source, item], z_recv.at[source, item], mp=me + step)
 
-        end = 0 if j < parts - 2 or item < 3 else 1
+        end = 0 if item < 3 else 1
 
         @pl.when((source < me) & (me < parts - 1 - end))
         def _():
@@ -280,7 +260,7 @@
 
     def keep(c):
         return pltpu.make_async_copy(
-            mine(mlp_chunk + c), piece(mlp_chunk + c, place, None), keep_sems.at[c]
+            mine(mlp_chunk + c), pieces_at(mlp_chunk + c, place, 1, None), keep_sems.at[c]
         )
 
     def small_copy(s):
@@ -314,9 +294,8 @@
         for c in range(width // UNIT):
             at = pl.ds(pl.multiple_of(u * UNIT + place * strip, 8), strip)
             copies.append((down_any.at[at, pl.ds(c * UNIT, UNIT)], pieces.at[u, 1, pl.ds(c * strip, strip), :]))
-    piece_copies = [pltpu.make_async_copy(a, b, piece_sems.at[i]) for i, (a, b) in enumerate(copies)]
-    for copy in piece_copies:
-        copy.start()
+    for source, target in copies:
+        pltpu.make_async_copy(source, target, piece_sem).start()
     greet(
         *[{"mp": lax.rem(me + s, parts)} for s in range(1, parts)],
         *[{"dp": flip(device, bit)} for bit in (1, 2, 4)],
@@ -336,7 +315,8 @@
 
     @pl.when(jnp.logical_not(inner))
     def _():
-        z_land[order[2]] = jnp.zeros(z_land.shape[1:], F32)
+        for source in order[1:]:
+            z_land[source] = jnp.zeros(z_land.shape[1:], F32)
 
     for j in range(2):
         bias_col[0, 2 * j * own : (2 * j + 1) * own, :] = small_land[me].T[:own, j : j + 1]
@@ -360,13 +340,17 @@
         value = ref[u, :HEAD_DIM, :].astype(F32)
         return jnp.max(jnp.sum(value * value, 0, keepdims=True), 1, keepdims=True)
 
-    def attend(at, r):
+    def project(at, r):
         tokens_r = pl.ds(pl.multiple_of(r * length, length), length)
         base = at * rows
         value = dot(w_low[at], h1_ref[tokens_r, :], NT) + bias_col[at]
         scale = HEAD_DIM**-0.5
         qkvt_ref[pl.ds(pl.multiple_of(base, own), own), tokens_r] = value[:own].astype(BF) * jnp.asarray(scale, BF)
         qkvt_ref[pl.ds(pl.multiple_of(base + own, own), 2 * own), tokens_r] = value[own:].astype(BF)
+
+    def attend(at, r):
+        tokens_r = pl.ds(pl.multiple_of(r * length, length), length)
+        base = at * rows
         same = row == seg_ref[pl.ds(r, 1), :]
         for u in range(heads):
             qx[u, HEAD_DIM:, :] = jnp.where(same | (row >= 8), 0.0, -BIG).astype(BF)
@@ -400,25 +384,21 @@
             landings(((0, 1), (1, 1)), ((0, 1),))
             spread.send(1)
         if n == 1:
-            for copy in piece_copies:
-                copy.wait()
+            spread.forward(0)
+            spread.forward(1)
             landings(((2, 0),), ((1, 0),))
             spread.send(2)
-            spread.forward(0)
+        if n == 1.5:
             landings(((2, 1),), ((1, 1),))
             spread.send(3)
-            own_copies(3, lambda copy: copy.start())
-            spread.forward(1)
         if n == 2:
+            spread.corner(0)
+            spread.corner(1)
+            spread.forward(2)
             landings(((0, 2), (1, 2)), ((2, 0),))
             spread.send(4)
-            spread.corner(0)
-            spread.forward(2)
-            landings((), ((2, 1),))
-            spread.send(5)
-            own_copies(4, lambda copy: copy.start())
-            spread.corner(1)
-            spread.forward(3)
+            pltpu.make_async_copy(pieces, pieces, piece_sem).wait()
+            own_copies(3, lambda copy: copy.start())
             for s in range(1, parts):
                 ref = small_land.at[lax.rem(me + s, parts)]
                 remote(ref, ref, small_send.at[0], small_recv.at[lax.rem(me + s, parts)], mp=me).wait_recv()
@@ -430,18 +410,23 @@
             spread.complete(0)
             spread.complete(1)
             at_place(1, land.at[order[0]])
+        if n == 2.5:
+            landings((), ((2, 1),))
+            spread.send(5)
+            spread.forward(3)
         if n == 3:
-            landings(((2, 2), (0, 3), (1, 3)), ((0, 2),))
+            spread.corner(2)
+            spread.corner(3)
+            spread.forward(4)
+            landings(((2, 2),), ((0, 2),))
             spread.send(w)
-            spread.corner(2)
-            spread.forward(4)
-            own_copies(5, lambda copy: copy.start())
-            spread.corner(3)
+            own_copies(4, lambda copy: copy.start())
+        if n == 3.5:
             spread.forward(5)
         if n == 4:
-            landings(((0, 4), (1, 4)), ((1, 2), (0, 3)))
+            landings(((0, 3), (1, 3)), ((1, 2), (0, 3)))
             spread.send(w + 1)
-            spread.send(m)
+            own_copies(5, lambda copy: copy.start())
             spread.corner(4)
             spread.corner(5)
             spread.forward(w)
@@ -449,35 +434,35 @@
             spread.complete(3)
             at_place(2, land.at[order[1]])
         if n == 5:
-            landings(((0, 5), (1, 5)), ((2, 2), (0, 4)))
+            landings(((0, 4), (1, 4)), ((2, 2), (0, 4)))
             spread.send(w + 2)
-            spread.send(m + 1)
+            for c in range(early):
+                spread.send(m + c)
             spread.corner(w)
             spread.forward(w + 1)
-            spread.forward(m)
         if n == 6:
-            landings(((2, 3), (2, 4)), ((0, 5), (1, 3)))
+            landings(((0, 5), (1, 5), (2, 3)), ((0, 5),))
             spread.forward(w + 2)
             spread.corner(w + 1)
-            spread.corner(m)
-            spread.forward(m + 1)
+            for c in range(early):
+                spread.forward(m + c)
             spread.complete(4)
             spread.complete(5)
             at_place(3, land.at[order[2]])
         if n == 7:
-            landings(((2, 5),), ((1, 4),))
+            landings(((2, 4),), ())
             spread.corner(w + 2)
-            spread.corner(m + 1)
+            for c in range(early):
+                keep(c).wait()
+                spread.corner(m + c)
             spread.complete(w)
-            spread.complete(m)
         if n == 8:
-            landings((), ((1, 5),))
+            landings(((2, 5),), ())
             z_copy.start()
             spread.complete(w + 1)
             spread.complete(w + 2)
-            spread.complete(m + 1)
             for c in range(early):
-                keep(c).wait()
+                spread.complete(m + c)
             land_copy.start()
             for j in range(parts - 1):
                 wo_low[(j + 1) * own : (j + 2) * own, :] = wo_land[order[j]].astype(BF)
@@ -488,6 +473,12 @@
 
     def step(n, carry):
         at, r = lax.div(n, 2), lax.rem(n, 2)
+        project(at, r)
+        for e in (1, 2, 3):
+            @pl.when(n == e)
+            def _():
+                event(e + 0.5)
+
         attend(at, r)
 
         @pl.when(r == 1)
@@ -565,7 +556,7 @@
             pltpu.VMEM((heads, wide, length), BF),
             pltpu.VMEM((heads, length, wide), BF),
             dma,
-            dma((units * (1 + width // UNIT),)),
+            dma,
             dma((EARLY,)),
             dma((5,)),
             dma((parts, 3)),
@@ -574,8 +565,8 @@
             dma((3 + units, 2)),
             dma((parts - 1,)),
             dma((parts,)),
-            dma((chunks, 9)),
-            dma((chunks, 9)),
+            dma((chunks,)),
+            dma((chunks, 3)),
         ],
         compiler_params=pltpu.CompilerParams(vmem_limit_bytes=62 * 2**20, collective_id=0, has_side_effects=True),
         name="front",
@@ -713,15 +704,23 @@
         if stage == 3:
             return [self.over(5, 4, self.one_piece, piece), self.over(6, 2, self.two_piece, piece)]
         if stage == 4:
-            return [self.over(7, 2, self.one, part), self.over(8, 4, self.two, part)]
+            return self.halves(0, self.one, self.two)
+        if stage == 4.5:
+            return self.halves(1, self.one, self.two)
         return [self.over(9, 1, self.base, self.half)]
+
+    def halves(self, h, one, two):
+        half = self.part // 2
+        return [self.over(7 + 3 * h, 2, one + h * half, half), self.over(8 + 3 * h, 4, two + h * half, half)]
 
     def arrivals(self, stage):
         part, piece = self.part, self.piece
         if stage == 3:
             return [self.over(5, 4, self.one_piece_away, piece), self.over(6, 2, self.two_piece_away, piece)]
         if stage == 4:
-            return [self.over(7, 2, self.one_away, part), self.over(8, 4, self.two_away, part)]
+            return self.halves(0, self.one_away, self.two_away)
+        if stage == 4.5:
+            return self.halves(1, self.one_away, self.two_away)
         if stage == 5:
             return [self.over(9, 1, self.away, self.half)]
         return self.copies(stage)
@@ -758,8 +757,8 @@
     def scratch(rows, width):
         dma = pltpu.SemaphoreType.DMA
         return [
-            dma((10,)),
-            dma((10,)),
+            dma((12,)),
+            dma((12,)),
             pltpu.VMEM((rows // 2, width), F32),
             pltpu.VMEM((rows // 8 + rows // 16, width), F32),
             pltpu.VMEM((rows // 8 + rows // 16, width), F32),
@@ -769,19 +768,21 @@
 def attend_back_kernel(
     seg_ref, qkv_ref, ot_ref, dt_ref, lse_ref, h1_any, main_any, tail_any,
     dqkv_ref, main_out, rest_out,
-    qx, kx, vx, dx, qn, dn, kn, acc, h1_ref, main_ref, rest_ref, whole_ref, in_sems, out_sems, main_send, main_recv, *comm,
+    qx, kx, vx, dx, qn, dn, kn, acc, h1_ref, part_ref, main_ref, rest_ref, whole_ref, in_sems, out_sems, main_send, main_recv, side_land, across_land,
+    *comm,
 ):
     step = pl.program_id(0)
     own, length = ot_ref.shape
     width = h1_ref.shape[1]
     heads = own // HEAD_DIM
     tail_at = rest_ref.shape[0] - tail_any.shape[0]
+    part = Total(part_ref, main_send, main_recv, None, side_land, across_land)
     main = Total(main_ref, main_send, main_recv)
     rest = Total(rest_ref, *comm)
     whole = Total(whole_ref, *comm[:2])
     loads = [
-        pltpu.make_async_copy(main_any.at[pl.ds(pl.multiple_of(at, 8), main.piece), :], main.rows(at, main.piece), sem)
-        for at, sem in ((main.one_piece, in_sems.at[0]), (main.two_piece, in_sems.at[1]))
+        pltpu.make_async_copy(main_any.at[pl.ds(pl.multiple_of(at, 8), part.part), :], part.rows(at, part.part), sem)
+        for at, sem in ((part.one, in_sems.at[0]), (part.two, in_sems.at[1]))
     ]
     loads.append(pltpu.make_async_copy(tail_any, rest_ref.at[pl.ds(tail_at, tail_any.shape[0]), :], in_sems.at[2]))
     loads.append(pltpu.make_async_copy(h1_any, h1_ref, in_sems.at[3]))
@@ -797,9 +798,17 @@
         greet(*[{"dp": flip(main.device, bit)} for bit in (1, 2, 4)])
         for copy in loads[:2]:
             copy.wait()
+        part.start(2)
+
+    @pl.when(step == 1)
+    def _():
+        part.finish(2)
+        for at in (part.one_piece, part.two_piece):
+            rows = pl.ds(pl.multiple_of(at, 8), part.piece)
+            main_ref[rows, :] = part_ref[rows, :]
         main.start(3)
 
-    @pl.when(step == 1)
+    @pl.when(step == 2)
     def _():
         main.finish(3)
         main.start(4)
@@ -808,13 +817,13 @@
     def _():
         rest.finish(0)
         rest.start(1)
-        main.finish(4)
-        main.start(5)
 
     @pl.when(step == 4)
     def _():
         rest.finish(1)
         rest.start(2)
+        main.finish(4)
+        main.start(4.5)
 
     @pl.when(step == 5)
     def _():
@@ -823,18 +832,22 @@
             rows = pl.ds(pl.multiple_of(at, 8), rest.piece)
             whole_ref[rows, :] = rest_ref[rows, :]
         whole.start(3)
+
+    @pl.when(step == 6)
+    def _():
+        whole.finish(3)
+        whole.start(4)
+        whole.start(4.5)
+        main.finish(4.5)
+        main.start(5)
+
+    @pl.when(step == 7)
+    def _():
+        whole.finish(4)
+        whole.finish(4.5)
+        whole.start(5)
         main.finish(5)
         stores[0].start()
-
-    @pl.when(step == 6)
-    def _():
-        whole.finish(3)
-        whole.start(4)
-
-    @pl.when(step == 7)
-    def _():
-        whole.finish(4)
-        whole.start(5)
 
     row = lax.broadcasted_iota(jnp.int32, (EXTRA, length), 0)
     same = row == seg_ref[pl.ds(jnp.where((step == 1) | (step >= 5), 1, 0), 1), :]
@@ -945,12 +958,15 @@
             pltpu.VMEM((heads, length, HEAD_DIM), F32),
             pltpu.VMEM((tokens, width), BF),
             pltpu.VMEM(main.shape, F32),
+            pltpu.VMEM(main.shape, F32),
             pltpu.VMEM((rest_rows, width), F32),
             pltpu.VMEM((rest_rows, width), F32),
             dma((4,)),
             dma((2,)),
-            dma((10,)),
-            dma((10,)),
+            dma((12,)),
+            dma((12,)),
+            pltpu.VMEM((main.shape[0] // 8 + main.shape[0] // 16, width), F32),
+            pltpu.VMEM((main.shape[0] // 8 + main.shape[0] // 16, width), F32),
         ]
         + Total.scratch(rest_rows, width),
         compiler_params=pltpu.CompilerParams(vmem_limit_bytes=60 * 2**20, collective_id=2, has_side_effects=True),
@@ -1039,82 +1055,72 @@
     )(dqkv, weights, x, mg, gains, main, rest, result)
 
 
-def sums_kernel(
-    in_ref, rest_any, gains_ref, shifts_ref, biases_ref, qv_bias_ref, up_bias_ref,
-    land, rows_v, rows_sem, sends, recvs, *, own, exchange,
-):
-    width = in_ref.shape[1]
-    at = 4 * own + 64
+def sums_kernel(in_ref, out_ref, land, sends, recvs):
+    device = lax.axis_index("dp")
+    place = lax.rem(device, 8)
+    others = []
+    for bits in range(1, 8):
+        other = device
+        for bit in (1, 2, 4):
+            if bits & bit:
+                other = flip(other, bit)
+        others.append(other)
+    greet(*[{"dp": other} for other in others])
+    copies = [
+        remote(in_ref, land.at[place], sends.at[i], recvs.at[place], dp=other) for i, other in enumerate(others)
+    ]
+    for copy in copies:
+        copy.start()
+    land[place] = in_ref[...]
+    for other in others:
+        peer = lax.rem(other, 8)
+        remote(in_ref, land.at[peer], sends.at[0], recvs.at[peer], dp=other).wait_recv()
+    out_ref[...] = jnp.sum(land[...], 0)
+    for copy in copies:
+        copy.wait_send()
+
+
+def add_sums(sums):
+    dma = pltpu.SemaphoreType.DMA
+    return pl.pallas_call(
+        sums_kernel,
+        in_specs=[WHOLE],
+        out_specs=WHOLE,
+        out_shape=shape_of(sums.shape, F32),
+        scratch_shapes=[pltpu.VMEM((8,) + sums.shape, F32), dma((7,)), dma((8,))],
+        compiler_params=pltpu.CompilerParams(collective_id=3, has_side_effects=True),
+        name="add_sums",
+    )(sums)
+
+
+def arrange_kernel(sums_ref, rest_any, gains_ref, shifts_ref, biases_ref, qv_bias_ref, up_bias_ref, rows_v, sems, *, own):
     loads = [
-        pltpu.make_async_copy(rest_any.at[pl.ds(low, 16), :], rows_v.at[i], rows_sem.at[i])
-        for i, low in enumerate((3 * own, at))
+        pltpu.make_async_copy(rest_any.at[pl.ds(low, 16), :], rows_v.at[i], sems.at[i])
+        for i, low in enumerate((3 * own, 4 * own + 64))
     ]
     for copy in loads:
         copy.start()
-    if exchange:
-        device = lax.axis_index("dp")
-        place = lax.rem(device, 8)
-        others = []
-        for bits in range(1, 8):
-            other = device
-            for bit in (1, 2, 4):
-                if bits & bit:
-                    other = flip(other, bit)
-            others.append(other)
-        greet(*[{"dp": other} for other in others])
-        copies = [
-            remote(in_ref, land.at[place], sends.at[i], recvs.at[place], dp=other) for i, other in enumerate(others)
-        ]
-        for copy in copies:
-            copy.start()
-        land[place] = in_ref[...]
+    gains_ref[0:1, :] = sums_ref[0:1, :]
+    shifts_ref[0:1, :] = sums_ref[1:2, :]
     for copy in loads:
         copy.wait()
-    small = rows_v[1]
-    biases_ref[...] = small[BIAS_ONE : BIAS_TWO + 1, :]
-    up_bias_ref[...] = small[UP_BIAS : UP_BIAS + 1, :]
+    gains_ref[1:2, :] = rows_v[1, GAIN_TWO : GAIN_TWO + 1, :]
+    shifts_ref[1:2, :] = rows_v[1, SHIFT_TWO : SHIFT_TWO + 1, :]
+    biases_ref[...] = rows_v[1, BIAS_ONE : BIAS_TWO + 1, :]
+    up_bias_ref[...] = rows_v[1, UP_BIAS, :]
     qv_bias_ref[0:1, :] = rows_v[0, 0:1, :own]
     qv_bias_ref[1:2, :] = rows_v[0, 8:9, :own]
-    gains_ref[1:2, :] = small[GAIN_TWO : GAIN_TWO + 1, :]
-    shifts_ref[1:2, :] = small[SHIFT_TWO : SHIFT_TWO + 1, :]
-    if exchange:
-        for other in others:
-            peer = lax.rem(other, 8)
-            remote(in_ref, land.at[peer], sends.at[0], recvs.at[peer], dp=other).wait_recv()
-        sums = jnp.sum(land[...], 0)
-    else:
-        sums = in_ref[...]
-    gains_ref[0:1, :] = sums[0:1, :]
-    shifts_ref[0:1, :] = sums[1:2, :]
-    if exchange:
-        for copy in copies:
-            copy.wait_send()
-
-
-def add_sums(sums, rest, own, exchange):
+
+
+def arrange(sums, rest, own):
     width = sums.shape[1]
-    dma = pltpu.SemaphoreType.DMA
-    options = dict(collective_id=3, has_side_effects=True) if exchange else {}
     return pl.pallas_call(
-        partial(sums_kernel, own=own, exchange=exchange),
+        partial(arrange_kernel, own=own),
         in_specs=[WHOLE, ANY],
         out_specs=[WHOLE] * 5,
-        out_shape=[
-            shape_of((2, width), F32),
-            shape_of((2, width), F32),
-            shape_of((2, width), F32),
-            shape_of((2, own), F32),
-            shape_of((1, width), F32),
-        ],
-        scratch_shapes=[
-            pltpu.VMEM((8,) + sums.shape, F32),
-            pltpu.VMEM((2, 16, width), F32),
-            dma((2,)),
-            dma((7,)),
-            dma((8,)),
-        ],
-        compiler_params=pltpu.CompilerParams(**options),
-        name="add_sums",
+        out_shape=[shape_of((2, width), F32)] * 3 + [shape_of((2, own), F32), shape_of((width,), F32)],
+        scratch_shapes=[pltpu.VMEM((2, 16, width), F32), pltpu.SemaphoreType.DMA((2,))],
+        name="arrange",
     )(sums, rest)
 
 
@@ -1136,7 +1142,7 @@
 def mlp_kernel(
     wo_ref, smalls_ref, bias_ref, gain_ref, shift_ref, x_any, ot_any, g_any, up_any, down_any, land_any, z_any,
     result_out, mg_out, dt_out, main_out, tail_out,
-    land, z_far, wide_w, own_w, g_ref, h2_ref, dt_ref, mine_ref, main_ref, tail_ref, mixed_ref, res_ref, hg_ref,
+    land, z_far, wide_w, own_w, g_ref, h2_ref, dt_ref, mine_ref, main_ref, tail_ref, normed_ref, inv_ref, res_ref, hg_ref,
     up_low, down_low, pre_s, ag_s,
     in_sems, w_sems, keep_sems, far_keep, far_send, far_recv, out_sems, tile_sems, send_sems, recv_sems, *comm,
 ):
@@ -1159,27 +1165,30 @@
         j = lax.div(c, units)
         return jnp.where(j == 0, order[0], jnp.where(j == 1, order[1], order[2]))
 
-    def piece(e, origin, half):
-        rows = pl.ds(pl.multiple_of(origin * share, 8), share)
+    def pieces_at(e, at, count, half):
+        rows = pl.ds(pl.multiple_of(at * share, 8), count * share)
         if half is None:
             return land.at[e, :, rows, :]
         return land.at[e, half, rows, :]
 
-    far_at = units * (parts - 2) - early
+    spread = Spread(pieces_at, send_sems, recv_sems)
+    far_at = units - early
+    far_count = units * (parts - 2)
 
     def mine(e):
-        if e >= far_at:
-            return z_far.at[e - far_at]
         return z_any.at[order[(early + e) // units], (early + e) % units]
 
     inner = (me > 0) & (me < parts - 1)
+
+    def far_source(u):
+        return z_any.at[jnp.where(u < units, order[1], order[2]), lax.rem(u, units)]
 
     def far_copy(u):
         step = jnp.where(lax.div(me, 2) == 0, -1, 1)
-        return remote(z_any.at[order[2], u], z_far.at[u], far_send.at[u], far_recv.at[u], mp=me + step)
+        return remote(far_source(u), z_far.at[u], far_send.at[u], far_recv.at[u], mp=me + step)
 
     def far_local(u):
-        return pltpu.make_async_copy(z_any.at[order[2], u], z_far.at[u], far_keep.at[u])
+        return pltpu.make_async_copy(far_source(u), z_far.at[u], far_keep.at[u])
 
     def far(u):
         @pl.when(inner)
@@ -1190,42 +1199,40 @@
         def _():
             remote(z_far.at[u], z_far.at[u], far_send.at[u], far_recv.at[u], mp=me).wait_recv()
 
-    spread = Spread(piece, send_sems, recv_sems, mine)
-
-    def keep(e):
-        return pltpu.make_async_copy(mine(e), piece(e, spread.place, None), keep_sems.at[e])
+    def keep(e, source):
+        return pltpu.make_async_copy(source, pieces_at(e, spread.at, 1, None), keep_sems.at[e])
+
+    def send(e):
+        @pl.when((e >= far_at) & (e < late))
+        def _():
+            far(e - far_at)
+            keep(e, z_far.at[e - far_at]).start()
+
+        @pl.when(e < late)
+        def _():
+            keep(e, z_far.at[0]).wait()
+            spread.send(e)
 
     def serve(n):
-        for e in range(late):
-            @pl.when(n == e)
-            def _():
-                if e >= far_at:
-                    far(e - far_at)
-                    keep(e).start()
-                spread.send(e)
-
-            @pl.when(n == e + 1)
-            def _():
-                spread.forward(e)
-
-            @pl.when(n == e + 2)
-            def _():
-                spread.corner(e)
+        send(n + 1)
+
+        @pl.when(n - 1 < late)
+        def _():
+            spread.forward(n - 1)
+
+        @pl.when((n > 1) & (n - 2 < late))
+        def _():
+            spread.corner(n - 2)
 
     def reduce(n):
         @pl.when(n == units)
         def _():
             total.start(0)
 
-        @pl.when(n == units + 5)
+        @pl.when(n == units + 7)
         def _():
             total.finish(0)
             total.start(1)
-
-        @pl.when(n == units + 8)
-        def _():
-            total.finish(1)
-            total.start(2)
 
     def unit(bias, grads_at):
         def front(i):
@@ -1275,11 +1282,11 @@
     for copy in own_load(0):
         copy.start()
     for e in range(far_at):
-        keep(e).start()
+        keep(e, mine(e)).start()
 
     @pl.when(inner)
     def _():
-        for u in range(units):
+        for u in range(far_count):
             far_local(u).start()
 
     greet(
@@ -1289,10 +1296,11 @@
 
     @pl.when(inner)
     def _():
-        for u in range(units):
+        for u in range(far_count):
             far_copy(u).start()
 
-    serve(0)
+    send(0)
+    send(1)
     main_ref[...] = jnp.zeros_like(main_ref)
     tail_ref[...] = jnp.zeros_like(tail_ref)
     for copy in loads[:2]:
@@ -1302,14 +1310,16 @@
     def first(i, carry):
         rows = pl.ds(pl.multiple_of(i * TILE, TILE), TILE)
         mixed = h2_ref[rows, :].astype(F32) + dot(dt_ref[:, rows], wo_ref[...], TN) + bias_ref[0:1, :]
-        mixed_ref[rows, :] = mixed
         res_ref[rows, :] = mixed + bias_ref[1:2, :]
         hg_ref[rows, :] = jnp.zeros((TILE, width), F32)
-        normed, _ = standardize(mixed)
+        normed, inv_std = standardize(mixed)
+        normed_ref[rows, :] = normed
+        inv_ref[rows, :] = inv_std
         h2_ref[rows, :] = (normed * gain_ref[1:2, :] + shift_ref[1:2, :]).astype(BF)
         return carry
 
-    lax.fori_loop(0, tiles, first, 0)
+    lax.fori_loop(0, tiles, first, 0, unroll=2)
+    serve(1)
     loads[2].wait()
 
     def own_unit(u, carry):
@@ -1328,7 +1338,7 @@
             chunk_load(0).start()
 
         unit(smalls_ref[me, 2:3, pl.ds(pl.multiple_of(u * UNIT, UNIT), UNIT)], u * UNIT)
-        serve(u + 1)
+        serve(u + 2)
         reduce(u + 1)
         return carry
 
@@ -1356,13 +1366,12 @@
         @pl.when(c >= early)
         def _():
             e = c - early
-            pltpu.make_async_copy(z_far.at[0], piece(e, spread.place, None), keep_sems.at[e]).wait()
             spread.complete(e)
             take(land, (e,))
 
         cols = pl.ds(pl.multiple_of(lax.rem(c, units) * UNIT, UNIT), UNIT)
         unit(smalls_ref[source_of(c), 2:3, cols], None)
-        serve(c + units + 1)
+        serve(c + units + 2)
         reduce(c + units + 1)
         return carry
 
@@ -1371,7 +1380,7 @@
     def tile_stores(i):
         rows = pl.ds(pl.multiple_of(i * TILE, TILE), TILE)
         return [
-            pltpu.make_async_copy(source, target, tile_sems.at[i, k])
+            pltpu.make_async_copy(source, target, tile_sems.at[k])
             for k, (source, target) in enumerate((
                 (h2_ref.at[rows, :], result_out.at[rows, :]),
                 (hg_ref.at[rows, :], mg_out.at[rows, :]),
@@ -1383,7 +1392,7 @@
         rows = pl.ds(pl.multiple_of(i * TILE, TILE), TILE)
         g = g_ref[rows, :].astype(F32)
         h2_ref[rows, :] = res_ref[rows, :].astype(BF)
-        normed, inv_std = standardize(mixed_ref[rows, :])
+        normed, inv_std = normed_ref[rows, :], inv_ref[rows, :]
         hg = hg_ref[rows, :]
         mg = g + norm_back(hg, normed, inv_std, gain_ref[1:2, :])
         hg_ref[rows, :] = mg
@@ -1396,11 +1405,11 @@
             copy.start()
         return carry
 
-    lax.fori_loop(0, tiles, finish, 0)
-    total.finish(2)
+    lax.fori_loop(0, tiles, finish, 0, unroll=2)
+    total.finish(1)
     ends = [
-        pltpu.make_async_copy(total.rows(at, total.piece), main_out.at[pl.ds(pl.multiple_of(at, 8), total.piece), :], sem)
-        for at, sem in ((total.one_piece, out_sems.at[0]), (total.two_piece, out_sems.at[1]))
+        pltpu.make_async_copy(total.rows(at, total.part), main_out.at[pl.ds(pl.multiple_of(at, 8), total.part), :], sem)
+        for at, sem in ((total.one, out_sems.at[0]), (total.two, out_sems.at[1]))
     ]
     ends.append(pltpu.make_async_copy(tail_ref, tail_out, out_sems.at[2]))
     for copy in ends:
@@ -1410,15 +1419,11 @@
 
     @pl.when(inner)
     def _():
-        for u in range(units):
+        for u in range(far_count):
             far_copy(u).wait_send()
 
-    def drain(i, carry):
-        for copy in tile_stores(i):
-            copy.wait()
-        return carry
-
-    lax.fori_loop(0, tiles, drain, 0)
+    for k, ref in enumerate((h2_ref, hg_ref, dt_ref)):
+        pltpu.make_async_copy(ref, ref, tile_sems.at[k]).wait()
     for copy in ends:
         copy.wait()
 
@@ -1448,7 +1453,7 @@
         ],
         scratch_shapes=[
             pltpu.VMEM((late, 2, width, UNIT), F32),
-            pltpu.VMEM((units, 2, width // 8, UNIT), F32),
+            pltpu.VMEM((units * (parts - 2), 2, width // 8, UNIT), F32),
             pltpu.VMEM((2, width, UNIT), F32),
             pltpu.VMEM((UNIT, width), F32),
             pltpu.VMEM((tokens, width), BF),
@@ -1458,6 +1463,7 @@
             pltpu.VMEM((rows, width), F32),
             pltpu.VMEM((tail, width), F32),
             pltpu.VMEM((tokens, width), F32),
+            pltpu.VMEM((tokens, 1), F32),
             pltpu.VMEM((tokens, width), F32),
             pltpu.VMEM((tokens, width), F32),
             pltpu.VMEM((width, UNIT), BF),
@@ -1467,13 +1473,13 @@
             dma((3,)),
             dma((2,)),
             dma((late,)),
-            dma((units,)),
-            dma((units,)),
-            dma((units,)),
+            dma((units * (parts - 2),)),
+            dma((units * (parts - 2),)),
+            dma((units * (parts - 2),)),
             dma((3,)),
-            dma((tiles, 3)),
-            dma((late, 9)),
-            dma((late, 9)),
+            dma((3,)),
+            dma((late,)),
+            dma((late, 3)),
         ]
         + Total.scratch(rows, width),
         compiler_params=pltpu.CompilerParams(vmem_limit_bytes=63 * 2**20, collective_id=1, has_side_effects=True),
@@ -1513,9 +1519,10 @@
     token_grad, sums_one, down_grad, up_grad, out_weight_grad, result, qkv_grad = token_back(
         dqkv, weights, tokens, mg, norm_gains, main, rest, result, ff, own
     )
+    sums_one = add_sums(sums_one)
     if dp_size > 8:
-        sums_one = lax.psum(sums_one, "dp")
-    gains_grad, shifts_grad, out_biases_grad, qv_bias_grad, up_bias_grad = add_sums(sums_one, rest, own, dp_size == 8)
+        sums_one = lax.psum(sums_one, "dp") / 8
+    gains_grad, shifts_grad, out_biases_grad, qv_bias_grad, up_bias_grad = arrange(sums_one, rest, own)
     return (
         result,
         token_grad,
@@ -1526,7 +1533,7 @@
         out_weight_grad,
         out_biases_grad,
         up_grad,
-        up_bias_grad.reshape(ff),
+        up_bias_grad,
         down_grad,
     )
 

time: 267 us -> 252 us (0.944)
  Pallas kernels: 260 us -> 250 us
  local copies, waits for them, and re-layouts: 5.05 us -> 0 us
    pallas_call x1, Pallas kernels: 94.7 us -> 87.3 us  [mlp(): pl.pallas_call(mlp_kernel, in_specs=[WHOLE] * 5 + [ANY] * 7, out_specs=[A...]
    unnamed x4 -> x0, local copies, waits for them, and re-layouts: 5.05 us -> none
    pallas_call x1, Pallas kernels: 72.3 us -> 67.5 us  [front(): pl.pallas_call(front_kernel, in_specs=[WHOLE] * 7 + [ANY] * 3, out_specs=...]
    pallas_call x1 -> x2, Pallas kernels: 7.33 us -> 9.48 us  [the longest x1 7.28 us: add_sums(): pl.pallas_call(sums_kernel, in_specs=[WHOLE], out_specs=WHOLE, out_shape=...]
where the time goes in v1:
time: 252 us; the launch traced here: 251 us
  Pallas kernels  250 us (99%)
    pallas_call x1, Pallas kernels, mlp(): pl.pallas_call(mlp_kernel, in_specs=[WHOLE] * 5 + [ANY] * 7, out_specs=[A...  87.3 us
    pallas_call x1, Pallas kernels, attend_back(): pl.pallas_call(attend_back_kernel, grid=(8,), in_specs=[ONCE, wide_block,...  67.7 us
    pallas_call x1, Pallas kernels, front(): pl.pallas_call(front_kernel, in_specs=[WHOLE] * 7 + [ANY] * 3, out_specs=...  67.5 us
    pallas_call x1, Pallas kernels, token_back(): pl.pallas_call(token_kernel, grid=(tokens // LONG_TILE,), in_specs=[col,...  17.5 us
    pallas_call x1, Pallas kernels, add_sums(): pl.pallas_call(sums_kernel, in_specs=[WHOLE], out_specs=WHOLE, out_shape=...  7.28 us

profile of v1, /device:TPU:0, one launch (start us, length us, event | category | flops | bytes accessed | tf_op | source)
XLA Modules:
  0.0 251.4 jit_solution(2545135217114002665)
XLA Ops:
  0.6 67.5 %front.1 = (f32[4,8,768]{2,1,0:T(8,128)}, f32[8,128]{1,0:T(8,128)}, bf16[2048,768]{1,0:T(8,128)(2,1)}, bf16[2304,768]{1,0:T(8,128)(2,1)}, bf16[768,768]{1,0:T(8,...) custom-call(f32[2,768]{1,0:T(2,128)} %gain_ref.5, ...), custom_call_target="tpu_custom_call" | custom-call | tf_op jit(solution)/shard_map/front/pallas_call | solution.py:523
  68.2 0.9 repair.1
  69.1 87.3 %mlp.1 = (bf16[2048,768]{1,0:T(8,128)(2,1)}, f32[2048,768]{1,0:T(8,128)}, bf16[768,2048]{1,0:T(8,128)(2,1)}, f32[1536,768]{1,0:T(8,128)}, f32[256,768]{1,0:T(8,128)}) custom-call(bf16[768,768]{1,0:T(8,128)(2,1)} %get-tuple-element.48.wo_ref, f32[4,8,768]{2,1,0:T(8,128)} %get-tuple-element.49.smalls_ref, f32[2,768]{1,0:T(2,128)} %bias_ref.1, ...), custom_call_target="tpu_custom_call" | custom-call | tf_op jit(solution)/shard_map/mlp/pallas_call | solution.py:1443
  156.4 67.7 %attend_back.1 = (bf16[2304,2048]{1,0:T(8,128)(2,1)}, f32[1536,768]{1,0:T(8,128)}, f32[896,768]{1,0:T(8,128)}) custom-call(s32[2,1024]{1,0:T(2,128)} %seg_ref.5, bf16[2304,2048]{1,0:T(8,128)(2,1)} %get-tuple-element.43.qkvt_any.qkv_ref, bf16[768,2048]{1,0:T(8,128)(2,1)} %get-tuple-element.47.ot_any.ot_ref, bf16[768,2048]{1,0:T(8,128)(2,1)} %get-tuple-element.52.dt_ref, ...), custom_call_target="tpu_custom_call" | custom-call | tf_op jit(solution)/shard_map/attend_back/pallas_call | solution.py:948
  224.1 17.5 %token_back.1 = (f32[2048,768]{1,0:T(8,128)}, f32[8,768]{1,0:T(8,128)}, f32[768,768]{1,0:T(8,128)}, f32[768,768]{1,0:T(8,128)}, f32[192,768]{1,0:T(8,128)}, /*in...) custom-call(bf16[2304,2048]{1,0:T(8,128)(2,1)} %get-tuple-element.57.dqkv_ref, bf16[2304,768]{1,0:T(8,128)(2,1)} %get-tuple-element.58.w_ref, ...), custom_call_target="tpu_custom_call" | custom-call | tf_op jit(solution)/shard_map/token_back/pallas_call | solution.py:1032
  241.7 7.3 %add_sums.1.sums_ref = f32[8,768]{1,0:T(8,128)} custom-call(f32[8,768]{1,0:T(8,128)} %get-tuple-element.65.in_ref), custom_call_target="tpu_custom_call" | custom-call | tf_op jit(solution)/shard_map/add_sums/pallas_call | solution.py:1085
  249.0 2.2 arrange.1

commit v2 on v1

--- a/solution.py
+++ b/solution.py
@@ -330,7 +330,7 @@
         h1_ref[at, :] = (normed * gain_ref[0:1, :] + shift_ref[0:1, :]).astype(BF)
         return carry
 
-    lax.fori_loop(0, tokens // TILE, norm_tile, 0)
+    lax.fori_loop(0, tokens // TILE, norm_tile, 0, unroll=2)
     h1_copy.start()
     row = lax.broadcasted_iota(jnp.int32, (EXTRA, length), 0)
     for u in range(heads):
@@ -394,11 +394,8 @@
         if n == 2:
             spread.corner(0)
             spread.corner(1)
-            spread.forward(2)
             landings(((0, 2), (1, 2)), ((2, 0),))
             spread.send(4)
-            pltpu.make_async_copy(pieces, pieces, piece_sem).wait()
-            own_copies(3, lambda copy: copy.start())
             for s in range(1, parts):
                 ref = small_land.at[lax.rem(me + s, parts)]
                 remote(ref, ref, small_send.at[0], small_recv.at[lax.rem(me + s, parts)], mp=me).wait_recv()
@@ -411,44 +408,48 @@
             spread.complete(1)
             at_place(1, land.at[order[0]])
         if n == 2.5:
+            spread.forward(2)
             landings((), ((2, 1),))
             spread.send(5)
             spread.forward(3)
+            pltpu.make_async_copy(pieces, pieces, piece_sem).wait()
+            own_copies(3, lambda copy: copy.start())
         if n == 3:
-            spread.corner(2)
-            spread.corner(3)
             spread.forward(4)
             landings(((2, 2),), ((0, 2),))
             spread.send(w)
             own_copies(4, lambda copy: copy.start())
         if n == 3.5:
+            spread.corner(2)
+            spread.corner(3)
             spread.forward(5)
         if n == 4:
+            spread.complete(2)
+            spread.complete(3)
+            at_place(2, land.at[order[1]])
             landings(((0, 3), (1, 3)), ((1, 2), (0, 3)))
             spread.send(w + 1)
             own_copies(5, lambda copy: copy.start())
+        if n == 4.5:
             spread.corner(4)
             spread.corner(5)
             spread.forward(w)
-            spread.complete(2)
-            spread.complete(3)
-            at_place(2, land.at[order[1]])
+            for c in range(early):
+                spread.send(m + c)
         if n == 5:
             landings(((0, 4), (1, 4)), ((2, 2), (0, 4)))
             spread.send(w + 2)
-            for c in range(early):
-                spread.send(m + c)
             spread.corner(w)
             spread.forward(w + 1)
         if n == 6:
+            spread.complete(4)
+            spread.complete(5)
+            at_place(3, land.at[order[2]])
             landings(((0, 5), (1, 5), (2, 3)), ((0, 5),))
             spread.forward(w + 2)
             spread.corner(w + 1)
             for c in range(early):
                 spread.forward(m + c)
-            spread.complete(4)
-            spread.complete(5)
-            at_place(3, land.at[order[2]])
         if n == 7:
             landings(((2, 4),), ())
             spread.corner(w + 2)
@@ -474,7 +475,7 @@
     def step(n, carry):
         at, r = lax.div(n, 2), lax.rem(n, 2)
         project(at, r)
-        for e in (1, 2, 3):
+        for e in (1, 2, 3, 4):
             @pl.when(n == e)
             def _():
                 event(e + 0.5)
@@ -1214,15 +1215,15 @@
             spread.send(e)
 
     def serve(n):
+        @pl.when(n - 1 < late)
+        def _():
+            spread.forward(n - 1)
+
         send(n + 1)
 
-        @pl.when(n - 1 < late)
-        def _():
-            spread.forward(n - 1)
-
-        @pl.when((n > 1) & (n - 2 < late))
-        def _():
-            spread.corner(n - 2)
+        @pl.when((n > 2) & (n - 3 < late))
+        def _():
+            spread.corner(n - 3)
 
     def reduce(n):
         @pl.when(n == units)

time: 252 us -> 247 us (0.980)
  Pallas kernels: 250 us -> 246 us
    pallas_call x1, Pallas kernels: 67.5 us -> 62.6 us  [front(): pl.pallas_call(front_kernel, in_specs=[WHOLE] * 7 + [ANY] * 3, out_specs=...]
    pallas_call x1, Pallas kernels: 67.7 us -> 71.2 us  [attend_back(): pl.pallas_call(attend_back_kernel, grid=(8,), in_specs=[ONCE, wide_block,...]
    pallas_call x1, Pallas kernels: 87.3 us -> 83.9 us  [mlp(): pl.pallas_call(mlp_kernel, in_specs=[WHOLE] * 5 + [ANY] * 7, out_specs=[A...]
where the time goes in v2:
time: 247 us; the launch traced here: 246 us
  Pallas kernels  246 us (100%)
    pallas_call x1, Pallas kernels, mlp(): pl.pallas_call(mlp_kernel, in_specs=[WHOLE] * 5 + [ANY] * 7, out_specs=[A...  83.9 us
    pallas_call x1, Pallas kernels, attend_back(): pl.pallas_call(attend_back_kernel, grid=(8,), in_specs=[ONCE, wide_block,...  71.2 us
    pallas_call x1, Pallas kernels, front(): pl.pallas_call(front_kernel, in_specs=[WHOLE] * 7 + [ANY] * 3, out_specs=...  62.6 us
    pallas_call x1, Pallas kernels, token_back(): pl.pallas_call(token_kernel, grid=(tokens // LONG_TILE,), in_specs=[col,...  17.5 us
    pallas_call x1, Pallas kernels, add_sums(): pl.pallas_call(sums_kernel, in_specs=[WHOLE], out_specs=WHOLE, out_shape=...  7.28 us

profile of v2, /device:TPU:0, one launch (start us, length us, event | category | flops | bytes accessed | tf_op | source)
XLA Modules:
  0.0 246.4 jit_solution(5522382389859656447)
XLA Ops:
  0.6 62.6 %front.1 = (f32[4,8,768]{2,1,0:T(8,128)}, f32[8,128]{1,0:T(8,128)}, bf16[2048,768]{1,0:T(8,128)(2,1)}, bf16[2304,768]{1,0:T(8,128)(2,1)}, bf16[768,768]{1,0:T(8,...) custom-call(f32[2,768]{1,0:T(2,128)} %gain_ref.5, ...), custom_call_target="tpu_custom_call" | custom-call | tf_op jit(solution)/shard_map/front/pallas_call | solution.py:524
  63.2 0.9 repair.1
  64.1 83.9 %mlp.1 = (bf16[2048,768]{1,0:T(8,128)(2,1)}, f32[2048,768]{1,0:T(8,128)}, bf16[768,2048]{1,0:T(8,128)(2,1)}, f32[1536,768]{1,0:T(8,128)}, f32[256,768]{1,0:T(8,128)}) custom-call(bf16[768,768]{1,0:T(8,128)(2,1)} %get-tuple-element.48.wo_ref, f32[4,8,768]{2,1,0:T(8,128)} %get-tuple-element.49.smalls_ref, f32[2,768]{1,0:T(2,128)} %bias_ref.1, ...), custom_call_target="tpu_custom_call" | custom-call | tf_op jit(solution)/shard_map/mlp/pallas_call | solution.py:1444
  148.0 71.2 %attend_back.1 = (bf16[2304,2048]{1,0:T(8,128)(2,1)}, f32[1536,768]{1,0:T(8,128)}, f32[896,768]{1,0:T(8,128)}) custom-call(s32[2,1024]{1,0:T(2,128)} %seg_ref.5, bf16[2304,2048]{1,0:T(8,128)(2,1)} %get-tuple-element.43.qkvt_any.qkv_ref, bf16[768,2048]{1,0:T(8,128)(2,1)} %get-tuple-element.47.ot_any.ot_ref, bf16[768,2048]{1,0:T(8,128)(2,1)} %get-tuple-element.52.dt_ref, ...), custom_call_target="tpu_custom_call" | custom-call | tf_op jit(solution)/shard_map/attend_back/pallas_call | solution.py:949
  219.2 17.5 %token_back.1 = (f32[2048,768]{1,0:T(8,128)}, f32[8,768]{1,0:T(8,128)}, f32[768,768]{1,0:T(8,128)}, f32[768,768]{1,0:T(8,128)}, f32[192,768]{1,0:T(8,128)}, /*in...) custom-call(bf16[2304,2048]{1,0:T(8,128)(2,1)} %get-tuple-element.57.dqkv_ref, bf16[2304,768]{1,0:T(8,128)(2,1)} %get-tuple-element.58.w_ref, ...), custom_call_target="tpu_custom_call" | custom-call | tf_op jit(solution)/shard_map/token_back/pallas_call | solution.py:1033
  236.8 7.3 %add_sums.1.sums_ref = f32[8,768]{1,0:T(8,128)} custom-call(f32[8,768]{1,0:T(8,128)} %get-tuple-element.65.in_ref), custom_call_target="tpu_custom_call" | custom-call | tf_op jit(solution)/shard_map/add_sums/pallas_call | solution.py:1086
  244.1 2.2 arrange.1
